TPU v7x, 512 devices: a whole 4x8x8 slice. The times are simulated.
512 devices in a mesh: tmpl: 32 (over x, y_hi, core), stn: 16 (over y_lo, z).
Axes of the slice: x: 4, y: 8 (y_hi: 4, y_lo: 2; y = y_hi * 2 + y_lo), z: 8, core: 2. Of those that a mesh axis runs over, the one named last changes fastest.
Arguments:
- data: bfloat16 [2, 96, 3, 1024], P(None, 'stn', None, 'tmpl'), may hold values from -6 to 6
- waves: bfloat16 [96, 512, 3, 300], P('stn', 'tmpl'), may hold values from -6 to 6
- slot_group: int32 [96, 512, 1], P('stn', 'tmpl'), may hold values from 0 to 31; in each aligned block of 16 rows (0 to 15, 16 to 31, ..., all dimensions but the last counted through in order) at most 2 rows name the same one
- slot_local: int32 [96, 512], P('stn', 'tmpl'), may hold values from 0 to 255
- moveout: int32 [96, 512], P('stn', 'tmpl'), may hold values from 0 to 469
- chan_mask: int32 [96, 3], P('stn'), may hold values 0 or 1
Outputs:
- scores: float32 [2, 8192, 256], P(None, ('tmpl', 'stn'))
Inputs may be any that keep to these rules, and one draw needn't show every extreme that they name: `slot_group`: among the 16 slots k*16 to (k+1)*16 - 1 of one station, no template group is named more than 2 times.
All inputs are finite; a program needn't handle non-finite values. No bound on the sum of `chan_mask` on one device may be relied on, other than what follows from the above.
Results may differ from a plain program's by a relative error of at most 0.0029.
Values may be sent and summed in bfloat16 or wider, within the bound.
A program may use at most 128 MiB of HBM per device.

v0:
```python
import jax
import jax.numpy as jnp
from jax import lax
from jax.sharding import PartitionSpec as P

NK = 256
TPD = 16


epsilon = 1e-06


def hankel(series, tap_count, lag_count):
    width = series.shape[-1]
    repeats = (1,) * (series.ndim - 1) + (tap_count + 1,)
    tiled = jnp.tile(series, repeats)[..., : tap_count * (width + 1)]
    return tiled.reshape(series.shape[:-1] + (tap_count, width + 1))[..., :lag_count]


def shift_rows(values, offsets):
    lag_index = offsets[..., None] + jnp.arange(NK, dtype=jnp.int32)
    return jnp.take_along_axis(values, lag_index, axis=-1)


def body(data, waves, slot_group, slot_local, moveout, chan_mask):
    samples = lax.all_gather(data, "tmpl", axis=3, tiled=True)
    blocks, stations_here, components, width = samples.shape
    slots = waves.shape[1]
    tap_count = waves.shape[3]
    lag_count = width - tap_count + 1
    tmpl_count = lax.axis_size("tmpl")
    slot_most = max(2, 2 * slots // tmpl_count)
    capacity = stations_here * slot_most
    slot_total = tmpl_count * capacity
    per_group = TPD * lax.axis_size("stn")
    group_size = 2
    group_count = stations_here // group_size
    stacked_data = jnp.moveaxis(
        samples.reshape(blocks, group_count, group_size, components, width), 1, 0
    )
    stacked_waves = waves.reshape(group_count, group_size, slots, components, tap_count)
    stacked_mask = chan_mask.reshape(group_count, group_size, components).astype(jnp.float32)

    def correlate(inputs):
        station_data, station_waves, station_mask = inputs
        hankel_rows = hankel(station_data, tap_count, lag_count)
        squares = station_data.astype(jnp.float32) ** 2
        running = jnp.cumsum(squares, axis=-1)
        padded = jnp.concatenate(
            [jnp.zeros(running.shape[:-1] + (1,), jnp.float32), running], axis=-1
        )
        data_power = (
            padded[..., tap_count : tap_count + lag_count] - padded[..., :lag_count]
        ) / tap_count
        wave_power = (
            jnp.einsum(
                "spcj,spcj->spc", station_waves, station_waves, preferred_element_type=jnp.float32
            )
            / tap_count
        )
        numerator = jnp.einsum(
            "spcj,bscjk->spbck", station_waves, hankel_rows, preferred_element_type=jnp.float32
        )
        denominator = (
            tap_count
            * jnp.sqrt(wave_power + epsilon)[:, :, None, :, None]
            * jnp.sqrt(jnp.moveaxis(data_power, 0, 1) + epsilon)[:, None]
        )
        channel_sum = jnp.sum(
            numerator / denominator * station_mask[:, None, None, :, None], axis=3
        )
        scaled = channel_sum / jnp.maximum(jnp.sum(station_mask, axis=-1), 1.0)[:, None, None, None]
        return scaled.astype(jnp.bfloat16)

    row_count = stations_here * slots
    corr_rows = lax.map(correlate, (stacked_data, stacked_waves, stacked_mask)).reshape(
        row_count, blocks, lag_count
    )
    group_ids = slot_group[..., 0]
    same_group = group_ids[:, :, None] == group_ids[:, None, :]
    earlier = jnp.arange(slots)[None, :] < jnp.arange(slots)[:, None]
    slot_rank = jnp.sum((same_group & earlier[None]).astype(jnp.int32), axis=2)
    position = (
        group_ids * capacity
        + jnp.arange(stations_here, dtype=jnp.int32)[:, None] * slot_most
        + slot_rank
    ).reshape(row_count)
    local_ids = slot_local.reshape(row_count)
    shift_by = moveout.reshape(row_count)
    id_rows = jnp.full((slot_total,), -1, jnp.int32).at[position].set(local_ids)
    id_rows = jnp.broadcast_to(
        id_rows.reshape(tmpl_count, capacity, 1), (tmpl_count, capacity, blocks)
    )
    template_axis = jnp.arange(per_group, dtype=jnp.int32)
    offsets = jnp.broadcast_to(shift_by[:, None], (row_count, blocks))
    shifted = shift_rows(corr_rows, offsets)
    send_rows = jnp.zeros((slot_total, blocks, NK), jnp.bfloat16).at[position].set(shifted)
    send_rows = send_rows.reshape(tmpl_count, capacity, blocks, NK)
    values = lax.all_to_all(send_rows, "tmpl", split_axis=0, concat_axis=0, tiled=True)
    template_ids = lax.all_to_all(id_rows, "tmpl", split_axis=0, concat_axis=0, tiled=True)
    items = values.shape[2]
    accumulate_template_ids = template_ids.reshape(slot_total, items)
    onehot = (
        jnp.transpose(accumulate_template_ids)[:, None, :] == template_axis[None, :, None]
    ).astype(jnp.bfloat16)
    stack_sums = jnp.einsum(
        "btq,qbk->btk",
        onehot,
        values.reshape(slot_total, items, NK),
        preferred_element_type=jnp.float32,
    )
    counts = jnp.sum(onehot, axis=2, dtype=jnp.float32)
    stack_sums, counts = (stack_sums, counts)
    owned_sums, owned_counts = (
        lax.psum_scatter(stack_sums, "stn", scatter_dimension=1, tiled=True),
        lax.psum_scatter(counts, "stn", scatter_dimension=1, tiled=True),
    )
    return (
        jnp.sqrt(jnp.float32(tap_count))
        * owned_sums
        / jnp.sqrt(jnp.maximum(owned_counts, 1.0))[..., None]
    )


def solution(mesh):
    in_specs = (
        P(None, "stn", None, "tmpl"),
        P("stn", "tmpl", None, None),
        P("stn", "tmpl", None),
        P("stn", "tmpl"),
        P("stn", "tmpl"),
        P("stn", None),
    )
    out_specs = P(None, ("tmpl", "stn"), None)
    return jax.shard_map(body, mesh=mesh, in_specs=in_specs, out_specs=out_specs, check_vma=False)
```

profile of v0, /device:TPU:1, one launch (start us, length us, event | category | flops | bytes accessed | tf_op | source)
XLA Modules:
  0.0 864.0 jit_solution(11526672355706711706)
XLA Ops:
  6.5 0.7 copy.77
  7.2 0.7 multiply_reduce_fusion
  7.9 0.2 convert_reduce_fusion.1
  8.5 0.8 reshape.167
  9.3 0.9 scatter_custom_fusion
  10.3 0.6 broadcast_in_dim.21
  10.9 11.2 %all-to-all-start = ((s32[32,12,2]{1,2,0:T(2,128)}), s32[32,12,2]{1,2,0:T(2,128)S(1)}, u32[]{:S(2)}, u32[]{:S(2)}) async-start(s32[32,12,2]{1,2,0:T(2,128)} %broadcast_in_dim.21), calls=%async_computation | async-start | bytes 65536 | tf_op jit(solution)/shard_map/all_to_all | solution.py:100
  22.1 0.8 broadcast_in_dim_reshape.3
  22.9 0.3 fusion.30
  23.3 0.8 copy.41
  24.2 50.0 %all_gather.3 = bf16[2,6,3,1024]{1,0,2,3:T(2,128)(2,1)S(1)} all-gather(bf16[2,6,3,32]{1,0,2,3:T(2,128)(2,1)S(1)} %copy.41), channel_id=1, replica_groups=mesh['tmpl'=32,'stn'=16] {'tmpl'}, dimensions={3}, use_global_device_ids=true | all-gather | bytes 76032 | tf_op jit(solution)/shard_map/all_gather | solution.py:26
  74.2 2.1 copy.42
  76.3 0.7 convert_element_type.31
  77.1 152.6 %while.10 = (s32[]{:T(128)}, bf16[3,2,16,2,725]{4,3,2,1,0:T(2,128)(2,1)S(1)}, bf16[3,2,2,3,1024]{4,1,3,2,0:T(2,128)(2,1)S(1)}, bf16[3,2,16,3,300]{4,2,3,1,0:T(8,...) while((s32[]{:T(128)}, bf16[3,2,16,2,725]{4,3,2,1,0:T(2,128)(2,1)S(1)}, ...), condition=%wide.region_7.8_spmd, body=%wide.region_2.0_spmd.sunk | while | flops 85834096 | bytes 59822800 | solution.py:76
  77.2 3.4 reduce-window.12
  80.8 1.1 reduce-window.13
  82.2 3.9 tile.13
  86.2 9.1 %tile.14 = bf16[2,2,3,308224]{3,1,2,0:T(2,128)(2,1)} reshape(bf16[2,2,3,301,1024]{4,3,1,2,0:T(8,128)(2,1)} %tile.13) | data formatting | bytes 14794752 | tf_op jit(solution)/shard_map/while/body/eval_jaxpr/tile | solution.py:16
  95.3 7.4 slice.48
  102.8 21.2 %reshape.187 = bf16[2,2,3,300,1025]{4,3,1,2,0:T(8,128)(2,1)} reshape(bf16[2,2,3,307500]{3,1,2,0:T(2,128)(2,1)} %slice.48) | data formatting | bytes 14760000 | tf_op jit(solution)/shard_map/while/body/eval_jaxpr/reshape | solution.py:17
  124.2 3.5 fusion.47
  128.1 3.4 reduce-window.12
  131.7 1.1 reduce-window.13
  133.1 3.9 tile.13
  137.1 9.1 %tile.14 = bf16[2,2,3,308224]{3,1,2,0:T(2,128)(2,1)} reshape(bf16[2,2,3,301,1024]{4,3,1,2,0:T(8,128)(2,1)} %tile.13) | data formatting | bytes 14794752 | tf_op jit(solution)/shard_map/while/body/eval_jaxpr/tile | solution.py:16
  146.2 7.4 slice.48
  153.6 21.2 %reshape.187 = bf16[2,2,3,300,1025]{4,3,1,2,0:T(8,128)(2,1)} reshape(bf16[2,2,3,307500]{3,1,2,0:T(2,128)(2,1)} %slice.48) | data formatting | bytes 14760000 | tf_op jit(solution)/shard_map/while/body/eval_jaxpr/reshape | solution.py:17
  175.1 3.5 fusion.47
  178.9 3.4 reduce-window.12
  182.6 1.1 reduce-window.13
  184.0 3.9 tile.13
  187.9 9.1 %tile.14 = bf16[2,2,3,308224]{3,1,2,0:T(2,128)(2,1)} reshape(bf16[2,2,3,301,1024]{4,3,1,2,0:T(8,128)(2,1)} %tile.13) | data formatting | bytes 14794752 | tf_op jit(solution)/shard_map/while/body/eval_jaxpr/tile | solution.py:16
  197.1 7.4 slice.48
  204.5 21.2 %reshape.187 = bf16[2,2,3,300,1025]{4,3,1,2,0:T(8,128)(2,1)} reshape(bf16[2,2,3,307500]{3,1,2,0:T(2,128)(2,1)} %slice.48) | data formatting | bytes 14760000 | tf_op jit(solution)/shard_map/while/body/eval_jaxpr/reshape | solution.py:17
  225.9 3.5 fusion.47
  229.7 466.6 %gather_fusion = bf16[49152]{0:T(1024)(128)(2,1)S(1)} fusion(bf16[96,2,725]{2,1,0:T(2,128)(2,1)S(1)} %bitcast.75, s32[49152]{0:T(1024)S(1)} %bitcast.76), kind=kCustom, calls=%fused_computation | custom fusion | bytes 786432 | tf_op jit(solution)/shard_map/jit(take_along_axis)/gather | solution.py:22
  696.3 0.3 and_select_fusion
  696.7 0.9 broadcast_in_dim.22
  697.6 10.8 %scatter_fusion = bf16[384,2,256]{2,1,0:T(2,128)(2,1)} fusion(bf16[384,2,256]{2,1,0:T(2,128)(2,1)} %broadcast_in_dim.22, s32[96]{0:T(128)S(1)} %fusion.33, bf16[96,2,256]{2,1,0:T(2,128)(2,1)S(1)} %and_select_fusion), kind=kCustom, calls=%fused_computation.2 | custom fusion | bytes 295296 | tf_op jit(solution)/shard_map/scatter | solution.py:97
  708.4 3.7 all-to-all-start.1
  712.3 0.2 convert_reduce_fusion
  712.5 0.8 copy.52
  713.4 14.4 %all-to-all-done.1 = bf16[32,12,2,256]{3,2,1,0:T(2,128)(2,1)S(1)} async-done(((bf16[32,12,2,256]{3,2,1,0:T(2,128)(2,1)}), bf16[32,12,2,256]{3,2,1,0:T(2,128)(2,1)S(1)}, u32[]{:S(2)}, u32[]{:S(2)}) %all-to-all-start.1) | async-done | bytes 393248 | tf_op jit(solution)/shard_map/all_to_all | solution.py:99
  727.8 1.1 fusion.24
  728.9 53.9 %reduce-scatter.7.cloned.1.call-done = f32[16,2]{1,0:T(8,128)} async-done(((f32[256,2]{1,0:T(8,128)}), f32[16,2]{1,0:T(8,128)}) %reduce-scatter.7.cloned.1.call-update) | async-done | bytes 144
  782.8 0.8 copy.53
  783.5 72.2 %reduce-scatter.5.cloned.1.call-done = f32[2,16,256]{2,1,0:T(8,128)} async-done(((f32[2,256,256]{2,1,0:T(8,128)}), f32[2,16,256]{2,1,0:T(8,128)}) %reduce-scatter.5.cloned.1.call-update) | async-done | bytes 32784 | tf_op jit(solution)/shard_map/reduce_scatter | solution.py:115
  855.7 1.4 multiply_divide_fusion
  (84 shorter events, 4.1 us)
Async XLA Ops:
  10.9 697.5 %all-to-all-start = ((s32[32,12,2]{1,2,0:T(2,128)}), s32[32,12,2]{1,2,0:T(2,128)S(1)}, u32[]{:S(2)}, u32[]{:S(2)}) async-start(s32[32,12,2]{1,2,0:T(2,128)} %broadcast_in_dim.21), calls=%async_computation | async-start | bytes 65536 | tf_op jit(solution)/shard_map/all_to_all | solution.py:100
  102.8 21.2 %copy-start = (bf16[3,2,16,3,300]{4,2,3,1,0:T(8,128)(2,1)S(1)}, bf16[3,2,16,3,300]{4,2,3,1,0:T(8,128)(2,1)}, u32[]{:S(2)}) copy-start(bf16[3,2,16,3,300]{4,2,3,1,0:T(8,128)(2,1)} %get-tuple-element.112) | copy-start | bytes 518404 | tf_op jit(solution)/shard_map/while
  153.6 21.2 %copy-start = (bf16[3,2,16,3,300]{4,2,3,1,0:T(8,128)(2,1)S(1)}, bf16[3,2,16,3,300]{4,2,3,1,0:T(8,128)(2,1)}, u32[]{:S(2)}) copy-start(bf16[3,2,16,3,300]{4,2,3,1,0:T(8,128)(2,1)} %get-tuple-element.112) | copy-start | bytes 518404 | tf_op jit(solution)/shard_map/while
  204.5 21.2 %copy-start = (bf16[3,2,16,3,300]{4,2,3,1,0:T(8,128)(2,1)S(1)}, bf16[3,2,16,3,300]{4,2,3,1,0:T(8,128)(2,1)}, u32[]{:S(2)}) copy-start(bf16[3,2,16,3,300]{4,2,3,1,0:T(8,128)(2,1)} %get-tuple-element.112) | copy-start | bytes 518404 | tf_op jit(solution)/shard_map/while
  708.4 19.4 %all-to-all-start.1 = ((bf16[32,12,2,256]{3,2,1,0:T(2,128)(2,1)}), bf16[32,12,2,256]{3,2,1,0:T(2,128)(2,1)S(1)}, u32[]{:S(2)}, u32[]{:S(2)}) async-start(bf16[32,12,2,256]{3,2,1,0:T(2,128)(2,1)} %bitcast.15), calls=%async_computation.1 | async-start | bytes 786432 | tf_op jit(solution)/shard_map/all_to_all | solution.py:99
  712.2 70.6 %reduce-scatter.7.cloned.1.call-start = ((), (), s32[]{:S(2)}) async-start(), calls=%async_computation.5 | async-start | bytes 139264
  713.3 142.4 %reduce-scatter.5.cloned.1.call-start = ((), (), s32[]{:S(2)}) async-start(), calls=%async_computation.4 | async-start | bytes 557056 | tf_op jit(solution)/shard_map/reduce_scatter | solution.py:115
Sparse Core Ops, SparseCore 0:
  715.8 66.9 reduce-scatter.6
  785.8 69.8 reduce-scatter.4
where the time goes:
time: 876 us; the launch traced here: 864 us
  local copies, waits for them, and re-layouts  614 us (70%)
  waiting for transfers between devices  140 us (16%)
  blocking collectives  50 us (6%)
  other arithmetic  19.1 us (2%)
  starting transfers between devices  15 us (2%)
  between operations  13.5 us (2%)
  matrix products  11.6 us (1%)
    gather x2, local copies, waits for them, and re-layouts, shift_rows(): return jnp.take_along_axis(values, lag_index, axis=-1)  467 us
    reduce_scatter x1, waiting for transfers between devices, body(): lax.psum_scatter(stack_sums, 'stn', scatter_dimension=1, tiled=True)  72.2 us
    reshape x3, local copies, waits for them, and re-layouts, hankel(): tiled.reshape(series.shape[:-1] + (tap_count, width + 1))[..., :lag_count]  63.6 us
    unnamed x3, waiting for transfers between devices  53.9 us
    all_gather x1, blocking collectives, body(): samples = lax.all_gather(data, 'tmpl', axis=3, tiled=True)  50 us
    another operation x6, local copies, waits for them, and re-layouts, hankel(): tiled = jnp.tile(series, repeats)[..., :tap_count * (width + 1)]  39.3 us
    slice x3, local copies, waits for them, and re-layouts, hankel(): tiled = jnp.tile(series, repeats)[..., :tap_count * (width + 1)]  22.3 us
  transfers between devices with their start and end apart: 4, of which 3 were waited for; matrix products, arithmetic and copies ran while one was open for 74% of the time, Pallas kernels for 0%

commit v1 on v0

v1 whole, which is shorter than its diff:
```python
import functools

import jax
import jax.numpy as jnp
from jax import lax
from jax.experimental import pallas as pl
from jax.experimental.pallas import tpu as pltpu
from jax.sharding import PartitionSpec as P

NT = 32
NS = 16
TAPS = 300
EPS = 1e-06
MESH = pl.DeviceIdType.MESH
f32, bf16, i32 = jnp.float32, jnp.bfloat16, jnp.int32


def iota(shape, axis):
    return lax.broadcasted_iota(i32, shape, axis)


def left(x, by):
    by %= 128
    return x if by == 0 else pltpu.roll(x, 128 - by, axis=x.ndim - 1)


def next_block(x):
    half = (iota(x.shape, x.ndim - 1) >> 5) & 1
    return jnp.where(half == 0, left(x, 32), left(x, -31))


def split2(x):
    hi = x.astype(bf16)
    return hi, (x - hi.astype(f32)).astype(bf16)


def dot(a, b):
    return jnp.dot(a, b, preferred_element_type=f32)


def kernel(
    cm, dtile, w0, pk, gl, out,
    send_a, recv_a, wt, invw, tsel, pb, vb, z0, zf, ssc,
    send_b, recv_b, key, ob, acc, send_c, recv_c, send_k, recv_k, q,
    sa, ra, sb, rb, sc_, rc, sk, rk,
):
    me_t, me_n = lax.axis_index("tmpl"), lax.axis_index("stn")

    bar = pltpu.get_barrier_semaphore()

    def greet_t(j, _):
        pl.semaphore_signal(bar, inc=1, device_id={"tmpl": lax.rem(me_t + j, NT)}, device_id_type=MESH)
        return 0

    def greet_n(j, _):
        pl.semaphore_signal(bar, inc=1, device_id={"stn": lax.rem(me_n + j, NS)}, device_id_type=MESH)
        return 0

    lax.fori_loop(1, NT, greet_t, 0)
    lax.fori_loop(1, NS, greet_n, 0)

    lane = iota((96, 128), 1)
    packed = pk[...]
    mine = (lane >> 4) == lax.rem(me_t, 8)
    id_rows = jnp.where(mine & (((lane >> 2) & 3) == (packed & 3)), (packed >> 2) & 511, 0)
    pick = iota((512, 96), 0) == gl[3:4, 0:96]
    ids = dot(pick.astype(f32).astype(bf16), id_rows.astype(f32).astype(bf16))
    send_a[...] = (ids.reshape(NT, 16, 128) + dtile[...].astype(f32)[None]).astype(bf16)
    recv_a[me_t] = send_a[me_t]

    pl.semaphore_wait(bar, NT - 1 + NS - 1)

    def send_first(j, _):
        peer = lax.rem(me_t + j, NT)
        pltpu.make_async_remote_copy(
            src_ref=send_a.at[peer], dst_ref=recv_a.at[me_t], send_sem=sa, recv_sem=ra,
            device_id={"tmpl": peer}, device_id_type=MESH).start()
        return 0

    lax.fori_loop(1, NT, send_first, 0)

    def prepare(s, _):
        rows = pk[pl.ds(pl.multiple_of(s * 16, 16), 16), :]
        fine = (rows >> 11) & 31
        lane16 = iota((16, 128), 1)
        usable = [cm[s, c].astype(f32) for c in range(3)]
        total = usable[0] + usable[1] + usable[2]
        per = jnp.where(total > 2.5, 1.0 / 3.0, jnp.where(total > 1.5, 0.5, 1.0)) / TAPS
        for c in range(3):
            sc = s * 3 + c
            x = [w0[sc, :, 128 * j:128 * j + 128].astype(f32) for j in range(3)]
            power = jnp.sum(x[0] * x[0] + x[1] * x[1] + x[2] * x[2], axis=1, keepdims=True)
            invw[sc] = jnp.broadcast_to(lax.rsqrt(power / TAPS + EPS), (16, 128)) * (usable[c] * per)
            for bit in range(5):
                by = 1 << bit
                y = [pltpu.roll(v, by, axis=1) for v in x]
                wide = [jnp.where(lane16 >= by, y[j], y[j - 1] if j else 0.0) for j in range(3)]
                on = (fine & by) != 0
                x = [jnp.where(on, wide[j], x[j]) for j in range(3)]
            k0 = iota((16, 16, 128), 1)
            l3 = iota((16, 16, 128), 2)
            y = [
                pltpu.roll(jnp.broadcast_to(v[:, None, :], (16, 16, 128)), 0, axis=2, stride=1, stride_axis=1)
                for v in x
            ]
            for j in range(3):
                t = jnp.where(l3 >= k0, y[j], y[j - 1] if j else 0.0)
                wt[sc, :, 128 * j:128 * j + 128] = t.reshape(256, 128).astype(bf16)
        k0 = iota((16, 16, 128), 1)
        l3 = iota((16, 16, 128), 2)
        hit = (l3 & 63) == k0 + fine[:, None, :]
        tsel[s] = jnp.where(hit, 1.0, 0.0).reshape(256, 128).astype(bf16)
        return 0

    lax.fori_loop(0, 6, prepare, 0)

    for r in range(3):
        pb[r] = jnp.where(iota((512, 128), 0) == gl[r:r + 1, :], 1.0, 0.0).astype(bf16)

    pltpu.make_async_copy(send_a.at[pl.ds(0, NT - 1)], recv_a.at[pl.ds(0, NT - 1)], ra).wait()
    zf[...] = recv_a[...].astype(f32).reshape(512, 128)
    for g in range(3):
        rows = [zf[pl.ds(4 * g + bh, NT, stride=16), :] for bh in range(4)]
        z0[128 * g:128 * g + 128, :] = jnp.concatenate(rows, axis=0).T

    row = iota((512, 256), 0)
    col = iota((512, 256), 1)
    same = ((row >> 4) & 7) == ((col >> 4) & 7)
    k0, r, kind = row & 15, col & 15, row >> 7
    inside = jnp.where(
        kind == 0, (r >= k0).astype(i32),
        jnp.where(kind == 1, 1, jnp.where(kind == 2, (r < k0 + 12).astype(i32), (r < k0 - 4).astype(i32))))
    windows = jnp.where(same, inside, 0).astype(f32).astype(bf16)
    for g in range(3):
        z = z0[128 * g:128 * g + 128, :]
        hi, lo = split2(z * z)
        sums = dot(windows, jnp.concatenate([hi, lo], axis=0))
        suffix, whole, e1, e2 = (sums[128 * i:128 * i + 128] for i in range(4))
        b2 = whole + next_block(whole)
        b4 = b2 + left(b2, 1)
        b8 = b4 + left(b4, 2)
        b16 = b8 + left(b8, 4)
        power = suffix + left(e1, 9) + next_block(b16 + left(whole, 8) + left(e2, 9))
        v = lax.rsqrt(power / TAPS + EPS)
        parts = [split2(x) for x in (v, next_block(v), left(v, 1))]
        for k in range(8):
            sc = 8 * g + k
            if sc >= 18:
                break
            for e in range(3):
                for part in range(2):
                    vb[sc // 3, 64 * part + 16 * e:64 * part + 16 * e + 16, 128 * (sc % 3):128 * (sc % 3) + 128] = (
                        parts[e][part][16 * k:16 * k + 16])
            for part in range(2):
                vb[sc // 3, 64 * part + 48:64 * part + 64, 128 * (sc % 3):128 * (sc % 3) + 128] = (
                    jnp.zeros((16, 128), bf16))

    def pair(rr, _):
        lane16 = iota((16, 128), 1)
        pieces = [[None, None] for _ in range(4)]
        for s2 in range(2):
            s = rr * 2 + s2
            norm = dot(tsel[s], vb[s])
            total = None
            for c in range(3):
                sc = s * 3 + c
                z = z0[pl.ds(pl.multiple_of(sc * 16, 16), 16), :]
                z1 = next_block(z)
                lagged = jnp.concatenate(
                    [left(x, u) for u in range(12) for x in (z, z1)], axis=0).astype(bf16)
                numer = dot(wt[sc], lagged)
                scaled = norm[:, 128 * c:128 * c + 128].reshape(16, 16, 128) * invw[sc][:, None, :]
                term = numer.reshape(16, 16, 128) * scaled
                total = term if total is None else total + term
            ssc[s2] = total.reshape(256, 128)
            coarse = pk[pl.ds(pl.multiple_of(s * 16, 16), 16), :] >> 16
            for chunk in range(4):
                merged = None
                for low in range(4):
                    x = ssc[s2, pl.ds(4 * chunk + low, 16, stride=16), :]
                    for bit in range(4):
                        x = jnp.where((coarse & (1 << bit)) != 0, left(x, 1 << bit), x)
                    x = left(x, -8 * low)
                    merged = x if merged is None else jnp.where(((lane16 >> 3) & 3) == low, x, merged)
                pieces[chunk][s2] = merged
        corr = jnp.concatenate([x for two in pieces for x in two], axis=0).astype(bf16)
        send_b[rr] = dot(pb[rr], corr).astype(bf16).reshape(NT, 16, 128)
        recv_b[rr, me_t] = send_b[rr, me_t]

        def send_second(j, _):
            peer = lax.rem(me_t + j, NT)
            pltpu.make_async_remote_copy(
                src_ref=send_b.at[rr, peer], dst_ref=recv_b.at[rr, me_t], send_sem=sb.at[rr], recv_sem=rb.at[rr],
                device_id={"tmpl": peer}, device_id_type=MESH).start()
            return 0

        lax.fori_loop(1, NT, send_second, 0)
        return 0

    lax.fori_loop(0, 3, pair, 0)

    lane32 = iota((1, 128), 1)
    for rr in range(3):
        marks = zf[pl.ds(12 + rr, NT, stride=16), :]
        for u in range(4):
            mark = jnp.sum(marks[8 * u:8 * u + 8], axis=0, keepdims=True).astype(i32)
            key[4 * rr + u:4 * rr + u + 1, :] = jnp.where(mark > 0, (lane32 & 3) * 256 + mark - 1, -1)

    def onehot(n, _):
        line = iota((64, 128), 0)
        code = ((line >> 4) & 3) * 256 + (line & 15) + n * 16
        found = None
        start = pl.multiple_of(n * 64, 64)
        for rr in range(3):
            for u in range(4):
                hit = jnp.where(code == key[4 * rr + u:4 * rr + u + 1, :], 1.0, 0.0)
                ob[rr, pl.ds(start, 64), 128 * u:128 * u + 128] = hit.astype(bf16)
                found = hit[:16] if found is None else found + hit[:16]
        number = jnp.broadcast_to(jnp.sum(found, axis=1, keepdims=True), (16, 128)).astype(i32)
        parts = jnp.where(iota((16, 128), 1) < 64, number & 127, number >> 7)
        send_k[n] = parts.astype(f32).astype(bf16)
        return 0

    lax.fori_loop(0, NS, onehot, 0)
    recv_k[me_n] = send_k[me_n]

    def send_counts(j, _):
        peer = lax.rem(me_n + j, NS)
        pltpu.make_async_remote_copy(
            src_ref=send_k.at[peer], dst_ref=recv_k.at[me_n], send_sem=sk, recv_sem=rk,
            device_id={"stn": peer}, device_id_type=MESH).start()
        return 0

    lax.fori_loop(1, NS, send_counts, 0)

    k = iota((512, 512), 1)
    place = ((k >> 2) & 3) * 128 + (k >> 8) * 64 + ((k >> 4) & 1) * 32 + (k & 3) * 8 + ((k >> 5) & 7)
    q[...] = jnp.where(iota((512, 512), 0) == place, 1.0, 0.0).astype(bf16)

    for rr in range(2):
        pltpu.make_async_copy(send_b.at[rr, pl.ds(0, NT - 1)], recv_b.at[rr, pl.ds(0, NT - 1)], rb.at[rr]).wait()
        part = dot(ob[rr], recv_b[rr].reshape(512, 128))
        if rr == 0:
            acc[...] = part
        else:
            acc[...] += part
    pltpu.make_async_copy(send_b.at[2, pl.ds(0, NT - 1)], recv_b.at[2, pl.ds(0, NT - 1)], rb.at[2]).wait()
    part = acc[...] + dot(ob[2], recv_b[2].reshape(512, 128))
    send_c[...] = part.astype(bf16).reshape(NS, 64, 128)
    recv_c[me_n] = send_c[me_n]

    def send_stacks(j, _):
        peer = lax.rem(me_n + j, NS)
        pltpu.make_async_remote_copy(
            src_ref=send_c.at[peer], dst_ref=recv_c.at[me_n], send_sem=sc_, recv_sem=rc,
            device_id={"stn": peer}, device_id_type=MESH).start()
        return 0

    lax.fori_loop(1, NS, send_stacks, 0)

    pltpu.make_async_copy(send_k.at[pl.ds(0, NS - 1)], recv_k.at[pl.ds(0, NS - 1)], rk).wait()
    found = jnp.sum(recv_k[...].astype(f32), axis=0)
    found = jnp.where(iota((16, 128), 1) < 64, found, found * 128.0)
    found = found + left(found, 64)
    scale = jnp.sqrt(f32(TAPS)) * lax.rsqrt(jnp.maximum(found, 1.0))

    pltpu.make_async_copy(send_c.at[pl.ds(0, NS - 1)], recv_c.at[pl.ds(0, NS - 1)], rc).wait()
    y = jnp.sum(recv_c[...].astype(f32), axis=0).reshape(4, 16, 128) * scale[None]
    y = jnp.concatenate([y[0], y[1], y[2], y[3]], axis=1)
    hi, rest = y.astype(bf16), y - y.astype(bf16).astype(f32)
    mid, low = split2(rest)
    moved = dot(jnp.concatenate([hi, mid, low], axis=0), q[...])
    moved = moved[0:16] + moved[16:32] + moved[32:48]
    out[0] = moved[:, :256]
    out[1] = moved[:, 256:]

    pltpu.make_async_copy(send_a.at[pl.ds(0, NT - 1)], recv_a.at[pl.ds(0, NT - 1)], sa).wait()
    for rr in range(3):
        pltpu.make_async_copy(send_b.at[rr, pl.ds(0, NT - 1)], recv_b.at[rr, pl.ds(0, NT - 1)], sb.at[rr]).wait()
    pltpu.make_async_copy(send_k.at[pl.ds(0, NS - 1)], recv_k.at[pl.ds(0, NS - 1)], sk).wait()
    pltpu.make_async_copy(send_c.at[pl.ds(0, NS - 1)], recv_c.at[pl.ds(0, NS - 1)], sc_).wait()


def body(data, waves, slot_group, slot_local, moveout, chan_mask):
    d = jnp.pad(data.reshape(2, 18, 2, 16), ((0, 0), (0, 6), (0, 0), (0, 0)))
    d = d.reshape(2, 3, 8, 2, 16).transpose(1, 0, 3, 2, 4).reshape(12, 128)
    dtile = jnp.pad(d, ((0, 4), (0, 0)))
    w0 = jnp.pad(jnp.transpose(waves, (0, 2, 1, 3)).reshape(18, 16, TAPS), ((0, 0), (0, 0), (0, 384 - TAPS)))
    group = slot_group[..., 0]
    earlier = jnp.arange(16)[None, :] < jnp.arange(16)[:, None]
    rank = jnp.sum(((group[:, :, None] == group[:, None, :]) & earlier[None]).astype(i32), axis=2)
    station = jnp.arange(6, dtype=i32)[:, None]
    quarter = (station & 1) * 2 + rank
    pk = (moveout << 11) | ((slot_local + 1) << 2) | quarter
    pk = jnp.broadcast_to(pk.reshape(96, 1), (96, 128))
    where = (group * 16 + quarter * 4).reshape(3, 1, 32)
    where = (where + jnp.arange(4, dtype=i32)[None, :, None]).reshape(3, 128)
    first = (group * 16 + 12 + (station >> 1)).reshape(1, 96)
    gl = jnp.concatenate([where, jnp.pad(first, ((0, 0), (0, 32)), constant_values=-1)], axis=0)
    gl = jnp.pad(gl, ((0, 4), (0, 0)))
    vmem = pl.BlockSpec(memory_space=pltpu.VMEM)
    dma = pltpu.SemaphoreType.DMA
    return pl.pallas_call(
        kernel,
        out_shape=jax.ShapeDtypeStruct((2, 16, 256), f32),
        in_specs=[pl.BlockSpec(memory_space=pltpu.SMEM), vmem, vmem, vmem, vmem],
        out_specs=vmem,
        scratch_shapes=[
            pltpu.VMEM((NT, 16, 128), bf16),
            pltpu.VMEM((NT, 16, 128), bf16),
            pltpu.VMEM((18, 256, 384), bf16),
            pltpu.VMEM((18, 16, 128), f32),
            pltpu.VMEM((6, 256, 128), bf16),
            pltpu.VMEM((3, 512, 128), bf16),
            pltpu.VMEM((6, 128, 384), bf16),
            pltpu.VMEM((384, 128), f32),
            pltpu.VMEM((512, 128), f32),
            pltpu.VMEM((2, 256, 128), f32),
            pltpu.VMEM((3, NT, 16, 128), bf16),
            pltpu.VMEM((3, NT, 16, 128), bf16),
            pltpu.VMEM((16, 128), i32),
            pltpu.VMEM((3, 1024, 512), bf16),
            pltpu.VMEM((1024, 128), f32),
            pltpu.VMEM((NS, 64, 128), bf16),
            pltpu.VMEM((NS, 64, 128), bf16),
            pltpu.VMEM((NS, 16, 128), bf16),
            pltpu.VMEM((NS, 16, 128), bf16),
            pltpu.VMEM((512, 512), bf16),
            dma, dma, dma((3,)), dma((3,)), dma, dma, dma, dma,
        ],
        compiler_params=pltpu.CompilerParams(
            collective_id=0, has_side_effects=True, vmem_limit_bytes=48 * 2**20),
    )(chan_mask, dtile, w0, pk, gl)


def solution(mesh):
    in_specs = (
        P(None, "stn", None, "tmpl"),
        P("stn", "tmpl", None, None),
        P("stn", "tmpl", None),
        P("stn", "tmpl"),
        P("stn", "tmpl"),
        P("stn", None),
    )
    out_specs = P(None, ("tmpl", "stn"), None)
    return jax.shard_map(body, mesh=mesh, in_specs=in_specs, out_specs=out_specs, check_vma=False)
```

time: 876 us -> 54.8 us (0.06); the launches traced: 864 us -> 54.5 us
  local copies, waits for them, and re-layouts: 614 us -> 3.91 us
  waiting for transfers between devices: 140 us -> 0 us
  blocking collectives: 50 us -> 0 us
  Pallas kernels: 0 us -> 48.7 us
  other arithmetic: 19.1 us -> 1.79 us
  starting transfers between devices: 15 us -> 0 us
  between operations: 13.5 us -> 0.06 us
  matrix products: 11.6 us -> 0 us
    gather x2 -> x0, local copies, waits for them, and re-layouts: 467 us -> none  [shift_rows(): return jnp.take_along_axis(values, lag_index, axis=-1)]
    reduce_scatter x1 -> x0, waiting for transfers between devices: 72.2 us -> none  [body(): lax.psum_scatter(stack_sums, 'stn', scatter_dimension=1, tiled=True)]
    reshape x5 -> x2, local copies, waits for them, and re-layouts: 64.5 us -> 0.89 us  [the longest x1 0.8 us: body(): d = jnp.pad(data.reshape(2, 18, 2, 16), ((0, 0), (0, 6), (0, 0), (0, 0)))]
    unnamed x3 -> x0, waiting for transfers between devices: 53.9 us -> none
    all_gather x1 -> x0, blocking collectives: 50 us -> none  [body(): samples = lax.all_gather(data, 'tmpl', axis=3, tiled=True)]
    pallas_call x0 -> x1, Pallas kernels: none -> 48.7 us  [body(): pl.pallas_call(kernel, out_shape=jax.ShapeDtypeStruct((2, 16, 256), f32),...]
    another operation x16 -> x0, local copies, waits for them, and re-layouts: 40.1 us -> none  [the longest x6 39.3 us: hankel(): tiled = jnp.tile(series, repeats)[..., :tap_count * (width + 1)]]
    slice x9 -> x0, local copies, waits for them, and re-layouts: 23 us -> none  [the longest x3 22.3 us: hankel(): tiled = jnp.tile(series, repeats)[..., :tap_count * (width + 1)]]
  transfers between devices with their start and end apart: 4 -> 0, of which waited for: 3 -> 0; matrix products, arithmetic and copies ran while one was open for 74% -> 0% of each run, Pallas kernels for 0% -> 0%
where the time goes in v1:
time: 54.8 us; the launch traced here: 54.5 us
  Pallas kernels  48.7 us (89%)
  local copies, waits for them, and re-layouts  3.91 us (7%)
  other arithmetic  1.79 us (3%)
    pallas_call x1, Pallas kernels, body(): pl.pallas_call(kernel, out_shape=jax.ShapeDtypeStruct((2, 16, 256), f32),...  48.7 us
    unnamed x6, local copies, waits for them, and re-layouts  2.09 us

profile of v1, /device:TPU:1, one launch (start us, length us, event | category | flops | bytes accessed | tf_op | source)
XLA Modules:
  0.0 54.5 jit_solution(10681823284477504150)
XLA Ops:
  0.0 0.0 copy-start
  0.0 0.1 add.99
  0.1 0.1 add.100
  0.2 0.1 add.106
  0.3 0.1 add.112
  0.3 0.1 add.113
  0.4 0.8 %copy.13.cm = s32[6,3]{1,0:T(8,128)S(1)} copy(s32[6,3]{0,1:T(4,128)} %param.11) | data formatting | bytes 144 | tf_op args[5]
  1.2 0.7 %copy.17 = s32[6,16,1]{1,0,2:T(8,128)S(1)} copy(s32[6,16,1]{1,2,0:T(1,128)} %param.8) | data formatting | bytes 768
  1.9 0.2 convert_reduce_fusion
  2.1 0.1 reduce_sum.12
  2.2 0.8 %add_or_fusion = s32[6,16]{1,0:T(8,128)S(1)} fusion(s32[6,16]{1,0:T(8,128)S(1)} %convert_reduce_fusion, s32[6,16]{1,0:T(8,128)} %param.9, s32[6,16]{1,0:T(8,128)} %param.10, s32[6]{0:T(128)S(1)} %and_multiply_fusion.1), kind=kLoop, calls=%fused_computation.4 | loop fusion | flops 576 | bytes 1560 | tf_op jit(solution)/shard_map/or | solution.py:294
  3.0 0.1 broadcast_in_dim.4
  3.1 0.7 %multiply_reduce_fusion = (s32[6,16]{1,0:T(8,128)S(1)}, s32[6,16]{1,0:T(8,128)S(1)}) fusion(s32[6,16,1]{1,2,0:T(1,128)} %param.8), kind=kLoop, calls=%fused_computation.10 | loop fusion | flops 192 | bytes 1152 | tf_op jit(solution)/shard_map/mul | solution.py:296
  3.8 0.1 mul.42
  3.9 0.1 add.111
  4.0 0.1 add.104
  4.1 0.8 %reshape.97 = bf16[2,18,2,16]{3,2,0,1:T(2,128)(2,1)S(1)} reshape(bf16[2,6,3,32]{3,0,2,1:T(2,128)(2,1)} %param.6) | data formatting | bytes 4608 | tf_op jit(solution)/shard_map/reshape | solution.py:285
  4.9 0.1 reshape.99
  5.0 0.1 broadcast_in_dim.5.pk
  5.1 0.0 copy-done
  5.1 48.7 %shard_map.64 = f32[2,16,256]{2,1,0:T(8,128)S(1)} custom-call(s32[6,3]{1,0:T(8,128)S(1)} %copy.13.cm, bf16[16,128]{1,0:T(8,128)(2,1)S(1)} %pad.21.dtile, bf16[18,16,384]{2,1,0:T(8,128)(2,1)S(1)} %pad.22.w0, s32[96,128]{1,0:T(8,128)S(1)} %broadcast_in_dim.5.pk, s32[8,128]{1,0:T(8,128)S(1)} %pad.24.gl), custom_call_target="tpu_custom_call" | custom-call | tf_op jit(solution)/shard_map/pallas_call | solution.py:303
  53.9 0.6 %copy.19 = f32[2,16,256]{2,1,0:T(8,128)} copy(f32[2,16,256]{2,1,0:T(8,128)S(1)} %shard_map.64) | data formatting | bytes 65536
  (16 shorter events, 0.1 us)
Async XLA Ops:
  0.0 5.1 %copy-start = (bf16[6,16,3,300]{3,1,2,0:T(8,128)(2,1)S(1)}, bf16[6,16,3,300]{3,1,2,0:T(8,128)(2,1)}, u32[]{:S(2)}) copy-start(bf16[6,16,3,300]{3,1,2,0:T(8,128)(2,1)} %param.7) | copy-start | bytes 518404

commit v2 on v1

--- a/solution.py
+++ b/solution.py
@@ -38,57 +38,124 @@
     return jnp.dot(a, b, preferred_element_type=f32)
 
 
+def far_first(j):
+    return jnp.where(j < 2, 2 - j, 9 - 3 * j)
+
+
+def tmpl_peer(me, j):
+    y = far_first(j >> 3)
+    x = far_first((j >> 1) & 3)
+    return ((((me >> 3) + x) & 3) << 3) | ((((me >> 1) + y) & 3) << 1) | ((me + 1 + j) & 1)
+
+
+def stn_peer(me, j):
+    a = j >> 1
+    z = jnp.where((a & 1) == 1, 4 - ((a + 1) >> 1), 4 + (a >> 1))
+    return ((((me >> 3) + 1 + j) & 1) << 3) | ((me + z) & 7)
+
+
 def kernel(
-    cm, dtile, w0, pk, gl, out,
-    send_a, recv_a, wt, invw, tsel, pb, vb, z0, zf, ssc,
+    data_in, waves_in, group_in, local_in, move_in, mask_in, out,
+    data_v, w0, group_v, local_v, move_v, cm, pk, codes,
+    send_a, recv_a, wt, invw, tsel, pb, windows, z0, zf, ssc,
     send_b, recv_b, key, ob, acc, send_c, recv_c, send_k, recv_k, q,
-    sa, ra, sb, rb, sc_, rc, sk, rk,
+    si, sw, sa, ra, sb, rb, sc_, rc, sk, rk,
 ):
     me_t, me_n = lax.axis_index("tmpl"), lax.axis_index("stn")
+    small = [
+        pltpu.make_async_copy(data_in, data_v.at[pl.ds(0, 18)], si.at[0]),
+        pltpu.make_async_copy(group_in, group_v, si.at[1]),
+        pltpu.make_async_copy(local_in, local_v, si.at[2]),
+        pltpu.make_async_copy(move_in, move_v, si.at[3]),
+        pltpu.make_async_copy(mask_in, cm, si.at[4]),
+    ]
+    large = pltpu.make_async_copy(waves_in, w0, sw)
+    for copy in small:
+        copy.start()
+    large.start()
 
     bar = pltpu.get_barrier_semaphore()
 
     def greet_t(j, _):
-        pl.semaphore_signal(bar, inc=1, device_id={"tmpl": lax.rem(me_t + j, NT)}, device_id_type=MESH)
+        pl.semaphore_signal(bar, inc=1, device_id={"tmpl": tmpl_peer(me_t, j)}, device_id_type=MESH)
         return 0
 
     def greet_n(j, _):
-        pl.semaphore_signal(bar, inc=1, device_id={"stn": lax.rem(me_n + j, NS)}, device_id_type=MESH)
-        return 0
-
-    lax.fori_loop(1, NT, greet_t, 0)
-    lax.fori_loop(1, NS, greet_n, 0)
-
+        pl.semaphore_signal(bar, inc=1, device_id={"stn": stn_peer(me_n, j)}, device_id_type=MESH)
+        return 0
+
+    lax.fori_loop(0, NT - 1, greet_t, 0)
+    lax.fori_loop(0, NS - 1, greet_n, 0)
+    for copy in small:
+        copy.wait()
+
+    sub16, lane16s = iota((16, 16), 0), iota((16, 16), 1)
+    codes[...] = jnp.zeros((8, 128), i32)
+    for s in range(6):
+        group = jnp.broadcast_to(group_v[s], (16, 16))
+        column = jnp.sum(jnp.where(sub16 == lane16s, group, 0).astype(f32), axis=1, keepdims=True).astype(i32)
+        same = group == column
+        rank_rows = jnp.sum(jnp.where(same & (lane16s < sub16), 1.0, 0.0), axis=1, keepdims=True)
+        rank_lanes = jnp.sum(jnp.where(same & (sub16 < lane16s), 1.0, 0.0), axis=0, keepdims=True)
+        fields = (move_v[s:s + 1, :] << 11) | ((local_v[s:s + 1, :] + 1) << 2) | ((s & 1) * 2)
+        fields = jnp.where(sub16 == lane16s, jnp.broadcast_to(fields, (16, 16)), 0)
+        fields = jnp.sum(fields.astype(f32), axis=1, keepdims=True) + rank_rows
+        pk[16 * s:16 * s + 16, :] = jnp.broadcast_to(fields, (16, 128)).astype(i32)
+        codes[s:s + 1, 0:16] = group_v[s] * 16 + ((s & 1) * 2 + rank_lanes.astype(i32)) * 4
+    spread = pltpu.roll(codes[...].astype(f32), 0, axis=1, stride=16, stride_axis=0)
+    code = jnp.sum(spread, axis=0, keepdims=True).astype(i32)
+
+    parts = []
+    row24, lane24 = iota((24, 128), 0), iota((24, 128), 1)
+    third = (row24 >= 6).astype(i32) + (row24 >= 12).astype(i32)
+    keep = ((lane24 >> 4) == row24 - 6 * third) & (row24 < 18)
+    for b in range(2):
+        samples = data_v[:, b, :]
+        for half in range(2):
+            widen = iota((32, 128), 0) == half * 16 + (iota((32, 128), 1) & 15)
+            parts.append(jnp.where(keep, dot(samples, jnp.where(widen, 1.0, 0.0).astype(bf16)), 0.0))
+    source = iota((16, 128), 1)
+    dest = iota((16, 128), 0)
+    bh = (source >= 24).astype(i32) + (source >= 48).astype(i32) + (source >= 72).astype(i32)
+    sc24 = source - 24 * bh
+    gather = dest == ((sc24 >= 6).astype(i32) + (sc24 >= 12).astype(i32)) * 4 + bh
+    gather = jnp.where(gather & (sc24 < 18) & (source < 96), 1.0, 0.0).astype(bf16)
+    stacked = jnp.concatenate(parts + [jnp.zeros((32, 128), f32)], axis=0).astype(bf16)
+    dtile = dot(gather, stacked)
     lane = iota((96, 128), 1)
     packed = pk[...]
-    mine = (lane >> 4) == lax.rem(me_t, 8)
+    mine = (lane >> 4) == (me_t & 7)
     id_rows = jnp.where(mine & (((lane >> 2) & 3) == (packed & 3)), (packed >> 2) & 511, 0)
-    pick = iota((512, 96), 0) == gl[3:4, 0:96]
-    ids = dot(pick.astype(f32).astype(bf16), id_rows.astype(f32).astype(bf16))
-    send_a[...] = (ids.reshape(NT, 16, 128) + dtile[...].astype(f32)[None]).astype(bf16)
+    first = (code & -16) + 12 + (iota((1, 128), 1) >> 5)
+    pick = iota((512, 96), 0) == first[:, 0:96]
+    ids = dot(jnp.where(pick, 1.0, 0.0).astype(bf16), id_rows.astype(f32).astype(bf16))
+    send_a[...] = (ids.reshape(NT, 16, 128) + dtile[None]).astype(bf16)
     recv_a[me_t] = send_a[me_t]
 
     pl.semaphore_wait(bar, NT - 1 + NS - 1)
 
     def send_first(j, _):
-        peer = lax.rem(me_t + j, NT)
+        peer = tmpl_peer(me_t, j)
         pltpu.make_async_remote_copy(
             src_ref=send_a.at[peer], dst_ref=recv_a.at[me_t], send_sem=sa, recv_sem=ra,
             device_id={"tmpl": peer}, device_id_type=MESH).start()
         return 0
 
-    lax.fori_loop(1, NT, send_first, 0)
+    lax.fori_loop(0, NT - 1, send_first, 0)
+
+    large.wait()
 
     def prepare(s, _):
         rows = pk[pl.ds(pl.multiple_of(s * 16, 16), 16), :]
         fine = (rows >> 11) & 31
         lane16 = iota((16, 128), 1)
-        usable = [cm[s, c].astype(f32) for c in range(3)]
+        usable = [cm[c, s].astype(f32) for c in range(3)]
         total = usable[0] + usable[1] + usable[2]
         per = jnp.where(total > 2.5, 1.0 / 3.0, jnp.where(total > 1.5, 0.5, 1.0)) / TAPS
         for c in range(3):
             sc = s * 3 + c
-            x = [w0[sc, :, 128 * j:128 * j + 128].astype(f32) for j in range(3)]
+            x = [w0[sc, :, 0:128].astype(f32), w0[sc, :, 128:256].astype(f32),
+                 jnp.pad(w0[sc, :, 256:TAPS].astype(f32), ((0, 0), (0, 384 - TAPS)))]
             power = jnp.sum(x[0] * x[0] + x[1] * x[1] + x[2] * x[2], axis=1, keepdims=True)
             invw[sc] = jnp.broadcast_to(lax.rsqrt(power / TAPS + EPS), (16, 128)) * (usable[c] * per)
             for bit in range(5):
@@ -114,15 +181,12 @@
 
     lax.fori_loop(0, 6, prepare, 0)
 
+    chunk_of = iota((1, 128), 1) >> 5
     for r in range(3):
-        pb[r] = jnp.where(iota((512, 128), 0) == gl[r:r + 1, :], 1.0, 0.0).astype(bf16)
-
-    pltpu.make_async_copy(send_a.at[pl.ds(0, NT - 1)], recv_a.at[pl.ds(0, NT - 1)], ra).wait()
-    zf[...] = recv_a[...].astype(f32).reshape(512, 128)
-    for g in range(3):
-        rows = [zf[pl.ds(4 * g + bh, NT, stride=16), :] for bh in range(4)]
-        z0[128 * g:128 * g + 128, :] = jnp.concatenate(rows, axis=0).T
-
+        placed = jnp.where(chunk_of == 0, left(code, 32 * r), 0)
+        placed = placed + left(placed, -32)
+        placed = placed + left(placed, -64) + chunk_of
+        pb[r] = jnp.where(iota((512, 128), 0) == placed, 1.0, 0.0).astype(bf16)
     row = iota((512, 256), 0)
     col = iota((512, 256), 1)
     same = ((row >> 4) & 7) == ((col >> 4) & 7)
@@ -130,11 +194,17 @@
     inside = jnp.where(
         kind == 0, (r >= k0).astype(i32),
         jnp.where(kind == 1, 1, jnp.where(kind == 2, (r < k0 + 12).astype(i32), (r < k0 - 4).astype(i32))))
-    windows = jnp.where(same, inside, 0).astype(f32).astype(bf16)
-    for g in range(3):
-        z = z0[128 * g:128 * g + 128, :]
+    windows[...] = jnp.where(same, inside, 0).astype(f32).astype(bf16)
+
+    pltpu.make_async_copy(send_a.at[pl.ds(0, NT - 1)], recv_a.at[pl.ds(0, NT - 1)], ra).wait()
+    zf[...] = recv_a[...].astype(f32).reshape(512, 128)
+
+    def pair(rr, _):
+        z0[...] = jnp.concatenate([zf[pl.ds(4 * rr + bh, NT, stride=16), :] for bh in range(4)], axis=0).T
+
+        z = z0[...]
         hi, lo = split2(z * z)
-        sums = dot(windows, jnp.concatenate([hi, lo], axis=0))
+        sums = dot(windows[...], jnp.concatenate([hi, lo], axis=0))
         suffix, whole, e1, e2 = (sums[128 * i:128 * i + 128] for i in range(4))
         b2 = whole + next_block(whole)
         b4 = b2 + left(b2, 1)
@@ -143,28 +213,23 @@
         power = suffix + left(e1, 9) + next_block(b16 + left(whole, 8) + left(e2, 9))
         v = lax.rsqrt(power / TAPS + EPS)
         parts = [split2(x) for x in (v, next_block(v), left(v, 1))]
-        for k in range(8):
-            sc = 8 * g + k
-            if sc >= 18:
-                break
-            for e in range(3):
-                for part in range(2):
-                    vb[sc // 3, 64 * part + 16 * e:64 * part + 16 * e + 16, 128 * (sc % 3):128 * (sc % 3) + 128] = (
-                        parts[e][part][16 * k:16 * k + 16])
-            for part in range(2):
-                vb[sc // 3, 64 * part + 48:64 * part + 64, 128 * (sc % 3):128 * (sc % 3) + 128] = (
-                    jnp.zeros((16, 128), bf16))
-
-    def pair(rr, _):
+        blank = jnp.zeros((16, 128), bf16)
+
         lane16 = iota((16, 128), 1)
         pieces = [[None, None] for _ in range(4)]
         for s2 in range(2):
             s = rr * 2 + s2
-            norm = dot(tsel[s], vb[s])
+            columns = []
+            for c in range(3):
+                at = 16 * (3 * s2 + c)
+                columns.append(jnp.concatenate(
+                    [x for part in range(2) for x in
+                     [parts[e][part][at:at + 16] for e in range(3)] + [blank]], axis=0))
+            norm = dot(tsel[s], jnp.concatenate(columns, axis=1))
             total = None
             for c in range(3):
                 sc = s * 3 + c
-                z = z0[pl.ds(pl.multiple_of(sc * 16, 16), 16), :]
+                z = z0[16 * (3 * s2 + c):16 * (3 * s2 + c) + 16, :]
                 z1 = next_block(z)
                 lagged = jnp.concatenate(
                     [left(x, u) for u in range(12) for x in (z, z1)], axis=0).astype(bf16)
@@ -188,13 +253,13 @@
         recv_b[rr, me_t] = send_b[rr, me_t]
 
         def send_second(j, _):
-            peer = lax.rem(me_t + j, NT)
+            peer = tmpl_peer(me_t, j)
             pltpu.make_async_remote_copy(
                 src_ref=send_b.at[rr, peer], dst_ref=recv_b.at[rr, me_t], send_sem=sb.at[rr], recv_sem=rb.at[rr],
                 device_id={"tmpl": peer}, device_id_type=MESH).start()
             return 0
 
-        lax.fori_loop(1, NT, send_second, 0)
+        lax.fori_loop(0, NT - 1, send_second, 0)
         return 0
 
     lax.fori_loop(0, 3, pair, 0)
@@ -225,13 +290,13 @@
     recv_k[me_n] = send_k[me_n]
 
     def send_counts(j, _):
-        peer = lax.rem(me_n + j, NS)
+        peer = stn_peer(me_n, j)
         pltpu.make_async_remote_copy(
             src_ref=send_k.at[peer], dst_ref=recv_k.at[me_n], send_sem=sk, recv_sem=rk,
             device_id={"stn": peer}, device_id_type=MESH).start()
         return 0
 
-    lax.fori_loop(1, NS, send_counts, 0)
+    lax.fori_loop(0, NS - 1, send_counts, 0)
 
     k = iota((512, 512), 1)
     place = ((k >> 2) & 3) * 128 + (k >> 8) * 64 + ((k >> 4) & 1) * 32 + (k & 3) * 8 + ((k >> 5) & 7)
@@ -245,18 +310,24 @@
         else:
             acc[...] += part
     pltpu.make_async_copy(send_b.at[2, pl.ds(0, NT - 1)], recv_b.at[2, pl.ds(0, NT - 1)], rb.at[2]).wait()
-    part = acc[...] + dot(ob[2], recv_b[2].reshape(512, 128))
-    send_c[...] = part.astype(bf16).reshape(NS, 64, 128)
+    last = recv_b[2].reshape(512, 128)
+    for i in range(4):
+        y = ((me_n >> 3) + 1 + i) & 1
+        z = (((me_n >> 2) & 1) + 1 + (i >> 1)) & 1
+        quarter = y * 2 + z
+        rows = pl.ds(pl.multiple_of(quarter * 256, 256), 256)
+        part = acc[rows, :] + dot(ob[2, rows, :], last)
+        send_c[pl.ds(quarter * 4, 4)] = part.astype(bf16).reshape(4, 64, 128)
+
+        def send_stacks(j, _):
+            peer = quarter * 4 + ((me_n + j) & 3)
+            pltpu.make_async_remote_copy(
+                src_ref=send_c.at[peer], dst_ref=recv_c.at[me_n], send_sem=sc_, recv_sem=rc,
+                device_id={"stn": peer}, device_id_type=MESH).start()
+            return 0
+
+        lax.fori_loop(1 if i == 3 else 0, 4, send_stacks, 0)
     recv_c[me_n] = send_c[me_n]
-
-    def send_stacks(j, _):
-        peer = lax.rem(me_n + j, NS)
-        pltpu.make_async_remote_copy(
-            src_ref=send_c.at[peer], dst_ref=recv_c.at[me_n], send_sem=sc_, recv_sem=rc,
-            device_id={"stn": peer}, device_id_type=MESH).start()
-        return 0
-
-    lax.fori_loop(1, NS, send_stacks, 0)
 
     pltpu.make_async_copy(send_k.at[pl.ds(0, NS - 1)], recv_k.at[pl.ds(0, NS - 1)], rk).wait()
     found = jnp.sum(recv_k[...].astype(f32), axis=0)
@@ -282,38 +353,31 @@
 
 
 def body(data, waves, slot_group, slot_local, moveout, chan_mask):
-    d = jnp.pad(data.reshape(2, 18, 2, 16), ((0, 0), (0, 6), (0, 0), (0, 0)))
-    d = d.reshape(2, 3, 8, 2, 16).transpose(1, 0, 3, 2, 4).reshape(12, 128)
-    dtile = jnp.pad(d, ((0, 4), (0, 0)))
-    w0 = jnp.pad(jnp.transpose(waves, (0, 2, 1, 3)).reshape(18, 16, TAPS), ((0, 0), (0, 0), (0, 384 - TAPS)))
-    group = slot_group[..., 0]
-    earlier = jnp.arange(16)[None, :] < jnp.arange(16)[:, None]
-    rank = jnp.sum(((group[:, :, None] == group[:, None, :]) & earlier[None]).astype(i32), axis=2)
-    station = jnp.arange(6, dtype=i32)[:, None]
-    quarter = (station & 1) * 2 + rank
-    pk = (moveout << 11) | ((slot_local + 1) << 2) | quarter
-    pk = jnp.broadcast_to(pk.reshape(96, 1), (96, 128))
-    where = (group * 16 + quarter * 4).reshape(3, 1, 32)
-    where = (where + jnp.arange(4, dtype=i32)[None, :, None]).reshape(3, 128)
-    first = (group * 16 + 12 + (station >> 1)).reshape(1, 96)
-    gl = jnp.concatenate([where, jnp.pad(first, ((0, 0), (0, 32)), constant_values=-1)], axis=0)
-    gl = jnp.pad(gl, ((0, 4), (0, 0)))
     vmem = pl.BlockSpec(memory_space=pltpu.VMEM)
+    hbm = pl.BlockSpec(memory_space=pltpu.HBM)
     dma = pltpu.SemaphoreType.DMA
     return pl.pallas_call(
         kernel,
         out_shape=jax.ShapeDtypeStruct((2, 16, 256), f32),
-        in_specs=[pl.BlockSpec(memory_space=pltpu.SMEM), vmem, vmem, vmem, vmem],
+        in_specs=[hbm] * 6,
         out_specs=vmem,
         scratch_shapes=[
+            pltpu.VMEM((24, 2, 32), bf16),
+            pltpu.VMEM((18, 16, TAPS), bf16),
+            pltpu.VMEM((6, 1, 16), i32),
+            pltpu.VMEM((6, 16), i32),
+            pltpu.VMEM((6, 16), i32),
+            pltpu.SMEM((3, 6), i32),
+            pltpu.VMEM((96, 128), i32),
+            pltpu.VMEM((8, 128), i32),
             pltpu.VMEM((NT, 16, 128), bf16),
             pltpu.VMEM((NT, 16, 128), bf16),
             pltpu.VMEM((18, 256, 384), bf16),
             pltpu.VMEM((18, 16, 128), f32),
             pltpu.VMEM((6, 256, 128), bf16),
             pltpu.VMEM((3, 512, 128), bf16),
-            pltpu.VMEM((6, 128, 384), bf16),
-            pltpu.VMEM((384, 128), f32),
+            pltpu.VMEM((512, 256), bf16),
+            pltpu.VMEM((128, 128), f32),
             pltpu.VMEM((512, 128), f32),
             pltpu.VMEM((2, 256, 128), f32),
             pltpu.VMEM((3, NT, 16, 128), bf16),
@@ -326,11 +390,16 @@
             pltpu.VMEM((NS, 16, 128), bf16),
             pltpu.VMEM((NS, 16, 128), bf16),
             pltpu.VMEM((512, 512), bf16),
-            dma, dma, dma((3,)), dma((3,)), dma, dma, dma, dma,
+            dma((5,)), dma, dma, dma, dma((3,)), dma((3,)), dma, dma, dma, dma,
         ],
         compiler_params=pltpu.CompilerParams(
-            collective_id=0, has_side_effects=True, vmem_limit_bytes=48 * 2**20),
-    )(chan_mask, dtile, w0, pk, gl)
+            collective_id=0, has_side_effects=True, vmem_limit_bytes=60 * 2**20),
+    )(
+        jnp.transpose(data, (1, 2, 0, 3)).reshape(18, 2, 32),
+        jnp.transpose(waves, (0, 2, 1, 3)).reshape(18, 16, TAPS),
+        jnp.transpose(slot_group, (0, 2, 1)),
+        slot_local, moveout, jnp.transpose(chan_mask),
+    )
 
 
 def solution(mesh):

time: 54.8 us -> 47.2 us (0.86)
  Pallas kernels: 48.7 us -> 45.6 us
  local copies, waits for them, and re-layouts: 3.91 us -> 1.38 us
  other arithmetic: 1.79 us -> 0 us
    pallas_call x1, Pallas kernels: 48.7 us -> 45.6 us  [body(): pl.pallas_call(kernel, out_shape=jax.ShapeDtypeStruct((2, 16, 256), f32),...]
    reshape x2 -> x0, local copies, waits for them, and re-layouts: 0.89 us -> none  [the longest x1 0.8 us: body(): d = jnp.pad(data.reshape(2, 18, 2, 16), ((0, 0), (0, 6), (0, 0), (0, 0)))]
    or x1 -> x0, other arithmetic: 0.78 us -> none  [body(): pk = moveout << 11 | slot_local + 1 << 2 | quarter]
    mul x3 -> x0, other arithmetic: 0.72 us -> none  [the longest x1 0.71 us: body(): where = (group * 16 + quarter * 4).reshape(3, 1, 32)]
    unnamed x6 -> x1, local copies, waits for them, and re-layouts: 2.09 us -> 1.38 us
    add x9 -> x0, local copies, waits for them, and re-layouts: 0.56 us -> none  [the longest x3 0.23 us: body(): first = (group * 16 + 12 + (station >> 1)).reshape(1, 96)]
where the time goes in v2:
time: 47.2 us; the launch traced here: 47 us
  Pallas kernels  45.6 us (97%)
  local copies, waits for them, and re-layouts  1.38 us (3%)
    pallas_call x1, Pallas kernels, body(): pl.pallas_call(kernel, out_shape=jax.ShapeDtypeStruct((2, 16, 256), f32),...  45.6 us
    unnamed x1, local copies, waits for them, and re-layouts  1.38 us

profile of v2, /device:TPU:1, one launch (start us, length us, event | category | flops | bytes accessed | tf_op | source)
XLA Modules:
  0.0 47.0 jit_solution(12388562202982204350)
XLA Ops:
  0.0 45.6 %shard_map.64 = f32[2,16,256]{2,1,0:T(8,128)} custom-call(bf16[18,2,32]{2,1,0:T(2,128)(2,1)} %bitcast.9, bf16[18,16,300]{2,1,0:T(8,128)(2,1)} %bitcast.8, s32[6,1,16]{2,1,0:T(1,128)} %bitcast.10, s32[6,16]{1,0:T(8,128)} %local_in.1, s32[6,16]{1,0:T(8,128)} %move_in.1, s32[3,6]{1,0:T(4,128)} %bitcast.11), custom_call_target="tpu_custom_call" | custom-call | tf_op jit(solution)/shard_map/pallas_call | solution.py:359
  45.6 1.4 %copy.8 = f32[2,16,256]{2,1,0:T(8,128)} copy(f32[2,16,256]{2,1,0:T(8,128)} %shard_map.64) | data formatting | bytes 65536

commit v3 on v2

--- a/solution.py
+++ b/solution.py
@@ -57,7 +57,7 @@
 def kernel(
     data_in, waves_in, group_in, local_in, move_in, mask_in, out,
     data_v, w0, group_v, local_v, move_v, cm, pk, codes,
-    send_a, recv_a, wt, invw, tsel, pb, windows, z0, zf, ssc,
+    send_a, recv_a, wt, invw, tsel, pb, windows, z0, zf, ssc, aligned, vb,
     send_b, recv_b, key, ob, acc, send_c, recv_c, send_k, recv_k, q,
     si, sw, sa, ra, sb, rb, sc_, rc, sk, rk,
 ):
@@ -125,8 +125,10 @@
     lane = iota((96, 128), 1)
     packed = pk[...]
     mine = (lane >> 4) == (me_t & 7)
-    id_rows = jnp.where(mine & (((lane >> 2) & 3) == (packed & 3)), (packed >> 2) & 511, 0)
-    first = (code & -16) + 12 + (iota((1, 128), 1) >> 5)
+    pair_of = iota((96, 128), 0) >> 5
+    spot = jnp.where(pair_of == 0, (lane & 15) >> 2, ((lane & 15) >> 1) + 4 - 4 * pair_of)
+    id_rows = jnp.where(mine & (spot == (packed & 3)), (packed >> 2) & 511, 0)
+    first = (code & -16) + 12 + (iota((1, 128), 1) >= 32).astype(i32)
     pick = iota((512, 96), 0) == first[:, 0:96]
     ids = dot(jnp.where(pick, 1.0, 0.0).astype(bf16), id_rows.astype(f32).astype(bf16))
     send_a[...] = (ids.reshape(NT, 16, 128) + dtile[None]).astype(bf16)
@@ -181,113 +183,134 @@
 
     lax.fori_loop(0, 6, prepare, 0)
 
-    chunk_of = iota((1, 128), 1) >> 5
-    for r in range(3):
-        placed = jnp.where(chunk_of == 0, left(code, 32 * r), 0)
-        placed = placed + left(placed, -32)
-        placed = placed + left(placed, -64) + chunk_of
-        pb[r] = jnp.where(iota((512, 128), 0) == placed, 1.0, 0.0).astype(bf16)
-    row = iota((512, 256), 0)
-    col = iota((512, 256), 1)
-    same = ((row >> 4) & 7) == ((col >> 4) & 7)
-    k0, r, kind = row & 15, col & 15, row >> 7
+    lane1 = iota((1, 128), 1)
+    placed = jnp.where(lane1 < 32, code, 0)
+    placed = placed + left(placed, -32)
+    placed = placed + left(placed, -64) + (lane1 >> 5)
+    pb[0] = jnp.where(iota((512, 128), 0) == placed, 1.0, 0.0).astype(bf16)
+    later = left(code, 32)
+    placed = jnp.where(lane1 < 64, (later & -16) + (lane1 >> 5) * 8 + ((later >> 2) & 3) * 2, 0)
+    placed = placed + left(placed, -64) + (lane1 >> 6)
+    pb[1] = jnp.where(iota((512, 128), 0) == placed, 1.0, 0.0).astype(bf16)
+    row = iota((288, 256), 0)
+    col = iota((288, 256), 1)
+    kind = (row >= 96).astype(i32) + (row >= 192).astype(i32)
+    row = row - 96 * kind
+    k0, r = row & 15, col & 15
     inside = jnp.where(
-        kind == 0, (r >= k0).astype(i32),
-        jnp.where(kind == 1, 1, jnp.where(kind == 2, (r < k0 + 12).astype(i32), (r < k0 - 4).astype(i32))))
-    windows[...] = jnp.where(same, inside, 0).astype(f32).astype(bf16)
+        kind == 0, (r >= k0).astype(i32), jnp.where(kind == 1, (r < k0 + 12).astype(i32), (r < k0 - 4).astype(i32)))
+    same = (row >> 4) == ((col >> 4) & 7)
+    windows[0:288, :] = jnp.where(same, inside, 0).astype(f32).astype(bf16)
+    same = iota((16, 256), 0) == ((iota((16, 256), 1) >> 4) & 7)
+    windows[288:304, :] = jnp.where(same, 1.0, 0.0).astype(bf16)
+
+    vb[:, 48:64, :] = jnp.zeros((6, 16, 384), bf16)
+    vb[:, 112:128, :] = jnp.zeros((6, 16, 384), bf16)
 
     pltpu.make_async_copy(send_a.at[pl.ds(0, NT - 1)], recv_a.at[pl.ds(0, NT - 1)], ra).wait()
     zf[...] = recv_a[...].astype(f32).reshape(512, 128)
 
+    sums = []
+    for rr in range(3):
+        z = jnp.concatenate([zf[pl.ds(4 * rr + bh, NT, stride=16), :] for bh in range(4)], axis=0).T
+        z0[rr] = z
+        hi, lo = split2(z * z)
+        sums.append(dot(windows[...], jnp.concatenate([hi, lo], axis=0)))
+    suffix, e1, e2 = (jnp.concatenate([x[96 * i:96 * i + 96] for x in sums], axis=0) for i in range(3))
+    whole = jnp.concatenate([x[288:296] for x in sums], axis=0)
+    b2 = whole + next_block(whole)
+    b4 = b2 + left(b2, 1)
+    b8 = b4 + left(b4, 2)
+    b16 = b8 + left(b8, 4)
+    middle = next_block(b16 + left(whole, 8))
+    middle = jnp.concatenate(
+        [jnp.broadcast_to(middle[8 * rr + k:8 * rr + k + 1], (16, 128)) for rr in range(3) for k in range(6)], axis=0)
+    half = (iota((288, 128), 1) >> 5) & 1
+    power = suffix + left(e1, 9) + (middle + jnp.where(half == 0, left(e2, 41), left(e2, -22)))
+    v = lax.rsqrt(power / TAPS + EPS)
+    for e, x in enumerate((v, next_block(v), left(v, 1))):
+        for part, y in enumerate(split2(x)):
+            for sc in range(18):
+                at = 64 * part + 16 * e
+                vb[sc // 3, at:at + 16, 128 * (sc % 3):128 * (sc % 3) + 128] = y[16 * sc:16 * sc + 16]
+
     def pair(rr, _):
-        z0[...] = jnp.concatenate([zf[pl.ds(4 * rr + bh, NT, stride=16), :] for bh in range(4)], axis=0).T
-
-        z = z0[...]
-        hi, lo = split2(z * z)
-        sums = dot(windows[...], jnp.concatenate([hi, lo], axis=0))
-        suffix, whole, e1, e2 = (sums[128 * i:128 * i + 128] for i in range(4))
-        b2 = whole + next_block(whole)
-        b4 = b2 + left(b2, 1)
-        b8 = b4 + left(b4, 2)
-        b16 = b8 + left(b8, 4)
-        power = suffix + left(e1, 9) + next_block(b16 + left(whole, 8) + left(e2, 9))
-        v = lax.rsqrt(power / TAPS + EPS)
-        parts = [split2(x) for x in (v, next_block(v), left(v, 1))]
-        blank = jnp.zeros((16, 128), bf16)
-
         lane16 = iota((16, 128), 1)
-        pieces = [[None, None] for _ in range(4)]
         for s2 in range(2):
             s = rr * 2 + s2
-            columns = []
-            for c in range(3):
-                at = 16 * (3 * s2 + c)
-                columns.append(jnp.concatenate(
-                    [x for part in range(2) for x in
-                     [parts[e][part][at:at + 16] for e in range(3)] + [blank]], axis=0))
-            norm = dot(tsel[s], jnp.concatenate(columns, axis=1))
+            norm = dot(tsel[s], vb[s])
             total = None
             for c in range(3):
                 sc = s * 3 + c
-                z = z0[16 * (3 * s2 + c):16 * (3 * s2 + c) + 16, :]
-                z1 = next_block(z)
-                lagged = jnp.concatenate(
-                    [left(x, u) for u in range(12) for x in (z, z1)], axis=0).astype(bf16)
+                z = z0[rr, 16 * (3 * s2 + c):16 * (3 * s2 + c) + 16, :]
+                z1 = next_block(z).astype(bf16)
+                z = z.astype(bf16)
+                lagged = jnp.concatenate([left(x, u) for u in range(12) for x in (z, z1)], axis=0)
                 numer = dot(wt[sc], lagged)
                 scaled = norm[:, 128 * c:128 * c + 128].reshape(16, 16, 128) * invw[sc][:, None, :]
                 term = numer.reshape(16, 16, 128) * scaled
                 total = term if total is None else total + term
-            ssc[s2] = total.reshape(256, 128)
-            coarse = pk[pl.ds(pl.multiple_of(s * 16, 16), 16), :] >> 16
+            ssc[s] = total.reshape(256, 128)
+            coarse = pk[pl.ds(pl.multiple_of(16 * s, 16), 16), :] >> 16
             for chunk in range(4):
                 merged = None
                 for low in range(4):
-                    x = ssc[s2, pl.ds(4 * chunk + low, 16, stride=16), :]
+                    x = ssc[s, pl.ds(4 * chunk + low, 16, stride=16), :].astype(bf16)
                     for bit in range(4):
                         x = jnp.where((coarse & (1 << bit)) != 0, left(x, 1 << bit), x)
                     x = left(x, -8 * low)
                     merged = x if merged is None else jnp.where(((lane16 >> 3) & 3) == low, x, merged)
-                pieces[chunk][s2] = merged
-        corr = jnp.concatenate([x for two in pieces for x in two], axis=0).astype(bf16)
-        send_b[rr] = dot(pb[rr], corr).astype(bf16).reshape(NT, 16, 128)
-        recv_b[rr, me_t] = send_b[rr, me_t]
+                aligned[chunk, pl.ds(pl.multiple_of(16 * s, 16), 16), :] = merged
+        return 0
+
+    def send(k, which, rows):
+        corr = jnp.concatenate(rows, axis=0)
+        send_b[k] = dot(pb[which], corr).astype(bf16).reshape(NT, 16, 128)
 
         def send_second(j, _):
             peer = tmpl_peer(me_t, j)
             pltpu.make_async_remote_copy(
-                src_ref=send_b.at[rr, peer], dst_ref=recv_b.at[rr, me_t], send_sem=sb.at[rr], recv_sem=rb.at[rr],
+                src_ref=send_b.at[k, peer], dst_ref=recv_b.at[k, me_t], send_sem=sb.at[k], recv_sem=rb.at[k],
                 device_id={"tmpl": peer}, device_id_type=MESH).start()
             return 0
 
-        lax.fori_loop(0, NT - 1, send_second, 0)
-        return 0
-
-    lax.fori_loop(0, 3, pair, 0)
-
-    lane32 = iota((1, 128), 1)
-    for rr in range(3):
-        marks = zf[pl.ds(12 + rr, NT, stride=16), :]
+        for j in range(NT - 1):
+            send_second(j, 0)
+        recv_b[k, me_t] = send_b[k, me_t]
+
+    lax.fori_loop(0, 1, pair, 0)
+    send(0, 0, [aligned[c, 0:32, :] for c in range(4)])
+    lax.fori_loop(1, 3, pair, 0)
+    for k in range(2):
+        send(1 + k, 1, [aligned[c, 32:96, :] for c in (2 * k, 2 * k + 1)])
+
+    for k in range(2):
+        marks = zf[pl.ds(12 + k, NT, stride=16), :]
         for u in range(4):
             mark = jnp.sum(marks[8 * u:8 * u + 8], axis=0, keepdims=True).astype(i32)
-            key[4 * rr + u:4 * rr + u + 1, :] = jnp.where(mark > 0, (lane32 & 3) * 256 + mark - 1, -1)
+            chunk = lane1 & (1 if k else 3)
+            key[4 * k + u:4 * k + u + 1, :] = jnp.where(mark > 0, chunk * 256 + mark - 1, -1)
 
     def onehot(n, _):
         line = iota((64, 128), 0)
-        code = ((line >> 4) & 3) * 256 + (line & 15) + n * 16
+        code = (line >> 4) * 256 + (line & 15) + n * 16
         found = None
-        start = pl.multiple_of(n * 64, 64)
-        for rr in range(3):
-            for u in range(4):
-                hit = jnp.where(code == key[4 * rr + u:4 * rr + u + 1, :], 1.0, 0.0)
-                ob[rr, pl.ds(start, 64), 128 * u:128 * u + 128] = hit.astype(bf16)
-                found = hit[:16] if found is None else found + hit[:16]
+        rows = pl.ds(pl.multiple_of(n * 32, 32), 32)
+        for u in range(4):
+            at = slice(128 * u, 128 * u + 128)
+            hit = jnp.where(code == key[u:u + 1, :], 1.0, 0.0)
+            ob[0, rows, at] = hit[:32].astype(bf16)
+            ob[1, rows, at] = hit[32:].astype(bf16)
+            found = hit[:16] if found is None else found + hit[:16]
+            hit = jnp.where(code[:32] == key[4 + u:5 + u, :], 1.0, 0.0)
+            ob[2, rows, at] = hit.astype(bf16)
+            found = found + hit[:16]
         number = jnp.broadcast_to(jnp.sum(found, axis=1, keepdims=True), (16, 128)).astype(i32)
         parts = jnp.where(iota((16, 128), 1) < 64, number & 127, number >> 7)
         send_k[n] = parts.astype(f32).astype(bf16)
         return 0
 
     lax.fori_loop(0, NS, onehot, 0)
-    recv_k[me_n] = send_k[me_n]
 
     def send_counts(j, _):
         peer = stn_peer(me_n, j)
@@ -297,37 +320,37 @@
         return 0
 
     lax.fori_loop(0, NS - 1, send_counts, 0)
+    recv_k[me_n] = send_k[me_n]
 
     k = iota((512, 512), 1)
     place = ((k >> 2) & 3) * 128 + (k >> 8) * 64 + ((k >> 4) & 1) * 32 + (k & 3) * 8 + ((k >> 5) & 7)
     q[...] = jnp.where(iota((512, 512), 0) == place, 1.0, 0.0).astype(bf16)
 
-    for rr in range(2):
-        pltpu.make_async_copy(send_b.at[rr, pl.ds(0, NT - 1)], recv_b.at[rr, pl.ds(0, NT - 1)], rb.at[rr]).wait()
-        part = dot(ob[rr], recv_b[rr].reshape(512, 128))
-        if rr == 0:
-            acc[...] = part
-        else:
-            acc[...] += part
-    pltpu.make_async_copy(send_b.at[2, pl.ds(0, NT - 1)], recv_b.at[2, pl.ds(0, NT - 1)], rb.at[2]).wait()
-    last = recv_b[2].reshape(512, 128)
-    for i in range(4):
-        y = ((me_n >> 3) + 1 + i) & 1
-        z = (((me_n >> 2) & 1) + 1 + (i >> 1)) & 1
-        quarter = y * 2 + z
-        rows = pl.ds(pl.multiple_of(quarter * 256, 256), 256)
-        part = acc[rows, :] + dot(ob[2, rows, :], last)
-        send_c[pl.ds(quarter * 4, 4)] = part.astype(bf16).reshape(4, 64, 128)
-
-        def send_stacks(j, _):
-            peer = quarter * 4 + ((me_n + j) & 3)
-            pltpu.make_async_remote_copy(
-                src_ref=send_c.at[peer], dst_ref=recv_c.at[me_n], send_sem=sc_, recv_sem=rc,
-                device_id={"stn": peer}, device_id_type=MESH).start()
-            return 0
-
-        lax.fori_loop(1 if i == 3 else 0, 4, send_stacks, 0)
-    recv_c[me_n] = send_c[me_n]
+    def arrived(k):
+        pltpu.make_async_copy(send_b.at[k, pl.ds(0, NT - 1)], recv_b.at[k, pl.ds(0, NT - 1)], rb.at[k]).wait()
+        return recv_b[k].reshape(512, 128)
+
+    stations = arrived(0)
+    for h in range(2):
+        acc[h] = dot(ob[h], stations)
+    for h in range(2):
+        stations = arrived(1 + h)
+        for i in range(2):
+            y = ((me_n >> 3) + 1 + i) & 1
+            rows = pl.ds(pl.multiple_of(y * 256, 256), 256)
+            part = acc[h, rows, :] + dot(ob[2, rows, :], stations)
+            send_c[h, pl.ds(y * 8, 8)] = part.astype(bf16).reshape(8, 32, 128)
+
+            def send_stacks(a, _):
+                z = jnp.where((a & 1) == 1, 4 - ((a + 1) >> 1), 4 + (a >> 1))
+                peer = y * 8 + ((me_n + z) & 7)
+                pltpu.make_async_remote_copy(
+                    src_ref=send_c.at[h, peer], dst_ref=recv_c.at[h, me_n], send_sem=sc_.at[h], recv_sem=rc.at[h],
+                    device_id={"stn": peer}, device_id_type=MESH).start()
+                return 0
+
+            lax.fori_loop(0, 7 if i == 1 else 8, send_stacks, 0)
+        recv_c[h, me_n] = send_c[h, me_n]
 
     pltpu.make_async_copy(send_k.at[pl.ds(0, NS - 1)], recv_k.at[pl.ds(0, NS - 1)], rk).wait()
     found = jnp.sum(recv_k[...].astype(f32), axis=0)
@@ -335,9 +358,12 @@
     found = found + left(found, 64)
     scale = jnp.sqrt(f32(TAPS)) * lax.rsqrt(jnp.maximum(found, 1.0))
 
-    pltpu.make_async_copy(send_c.at[pl.ds(0, NS - 1)], recv_c.at[pl.ds(0, NS - 1)], rc).wait()
-    y = jnp.sum(recv_c[...].astype(f32), axis=0).reshape(4, 16, 128) * scale[None]
-    y = jnp.concatenate([y[0], y[1], y[2], y[3]], axis=1)
+    ordered = []
+    for h in range(2):
+        pltpu.make_async_copy(send_c.at[h, pl.ds(0, NS - 1)], recv_c.at[h, pl.ds(0, NS - 1)], rc.at[h]).wait()
+        y = jnp.sum(recv_c[h].astype(f32), axis=0)
+        ordered += [y[:16] * scale, y[16:] * scale]
+    y = jnp.concatenate(ordered, axis=1)
     hi, rest = y.astype(bf16), y - y.astype(bf16).astype(f32)
     mid, low = split2(rest)
     moved = dot(jnp.concatenate([hi, mid, low], axis=0), q[...])
@@ -349,7 +375,8 @@
     for rr in range(3):
         pltpu.make_async_copy(send_b.at[rr, pl.ds(0, NT - 1)], recv_b.at[rr, pl.ds(0, NT - 1)], sb.at[rr]).wait()
     pltpu.make_async_copy(send_k.at[pl.ds(0, NS - 1)], recv_k.at[pl.ds(0, NS - 1)], sk).wait()
-    pltpu.make_async_copy(send_c.at[pl.ds(0, NS - 1)], recv_c.at[pl.ds(0, NS - 1)], sc_).wait()
+    for h in range(2):
+        pltpu.make_async_copy(send_c.at[h, pl.ds(0, NS - 1)], recv_c.at[h, pl.ds(0, NS - 1)], sc_.at[h]).wait()
 
 
 def body(data, waves, slot_group, slot_local, moveout, chan_mask):
@@ -358,7 +385,7 @@
     dma = pltpu.SemaphoreType.DMA
     return pl.pallas_call(
         kernel,
-        out_shape=jax.ShapeDtypeStruct((2, 16, 256), f32),
+        out_shape=pltpu.VMEM((2, 16, 256), f32),
         in_specs=[hbm] * 6,
         out_specs=vmem,
         scratch_shapes=[
@@ -375,22 +402,24 @@
             pltpu.VMEM((18, 256, 384), bf16),
             pltpu.VMEM((18, 16, 128), f32),
             pltpu.VMEM((6, 256, 128), bf16),
-            pltpu.VMEM((3, 512, 128), bf16),
-            pltpu.VMEM((512, 256), bf16),
-            pltpu.VMEM((128, 128), f32),
+            pltpu.VMEM((2, 512, 128), bf16),
+            pltpu.VMEM((304, 256), bf16),
+            pltpu.VMEM((3, 128, 128), f32),
             pltpu.VMEM((512, 128), f32),
-            pltpu.VMEM((2, 256, 128), f32),
+            pltpu.VMEM((6, 256, 128), f32),
+            pltpu.VMEM((4, 96, 128), bf16),
+            pltpu.VMEM((6, 128, 384), bf16),
             pltpu.VMEM((3, NT, 16, 128), bf16),
             pltpu.VMEM((3, NT, 16, 128), bf16),
             pltpu.VMEM((16, 128), i32),
-            pltpu.VMEM((3, 1024, 512), bf16),
-            pltpu.VMEM((1024, 128), f32),
-            pltpu.VMEM((NS, 64, 128), bf16),
-            pltpu.VMEM((NS, 64, 128), bf16),
+            pltpu.VMEM((3, 512, 512), bf16),
+            pltpu.VMEM((2, 512, 128), f32),
+            pltpu.VMEM((2, NS, 32, 128), bf16),
+            pltpu.VMEM((2, NS, 32, 128), bf16),
             pltpu.VMEM((NS, 16, 128), bf16),
             pltpu.VMEM((NS, 16, 128), bf16),
             pltpu.VMEM((512, 512), bf16),
-            dma((5,)), dma, dma, dma, dma((3,)), dma((3,)), dma, dma, dma, dma,
+            dma((5,)), dma, dma, dma, dma((3,)), dma((3,)), dma((2,)), dma((2,)), dma, dma,
         ],
         compiler_params=pltpu.CompilerParams(
             collective_id=0, has_side_effects=True, vmem_limit_bytes=60 * 2**20),

time: 47.2 us -> 45.7 us (0.968)
  local copies, waits for them, and re-layouts: 1.38 us -> 0.62 us
  Pallas kernels: 45.6 us -> 45 us
    unnamed x1, local copies, waits for them, and re-layouts: 1.38 us -> 0.62 us
    pallas_call x1, Pallas kernels: 45.6 us -> 45 us  [body(): pl.pallas_call(kernel, out_shape=pltpu.VMEM((2, 16, 256), f32), in_specs=...]
where the time goes in v3:
time: 45.7 us; the launch traced here: 45.6 us
  Pallas kernels  45 us (98%)
  local copies, waits for them, and re-layouts  0.62 us (1%)
    pallas_call x1, Pallas kernels, body(): pl.pallas_call(kernel, out_shape=pltpu.VMEM((2, 16, 256), f32), in_specs=...  45 us

profile of v3, /device:TPU:1, one launch (start us, length us, event | category | flops | bytes accessed | tf_op | source)
XLA Modules:
  0.0 45.6 jit_solution(7975283466753848951)
XLA Ops:
  0.0 45.0 %shard_map.64 = f32[2,16,256]{2,1,0:T(8,128)S(1)} custom-call(bf16[18,2,32]{2,1,0:T(2,128)(2,1)} %bitcast.9, bf16[18,16,300]{2,1,0:T(8,128)(2,1)} %bitcast.8, s32[6,1,16]{2,1,0:T(1,128)} %bitcast.10, s32[6,16]{1,0:T(8,128)} %local_in.1, s32[6,16]{1,0:T(8,128)} %move_in.1, s32[3,6]{1,0:T(4,128)} %bitcast.11), custom_call_target="tpu_custom_call" | custom-call | tf_op jit(solution)/shard_map/pallas_call | solution.py:386
  45.0 0.6 %copy.8 = f32[2,16,256]{2,1,0:T(8,128)} copy(f32[2,16,256]{2,1,0:T(8,128)S(1)} %shard_map.64) | data formatting | bytes 65536

commit v4 on v3

--- a/solution.py
+++ b/solution.py
@@ -38,20 +38,25 @@
     return jnp.dot(a, b, preferred_element_type=f32)
 
 
-def far_first(j):
-    return jnp.where(j < 2, 2 - j, 9 - 3 * j)
-
-
-def tmpl_peer(me, j):
-    y = far_first(j >> 3)
-    x = far_first((j >> 1) & 3)
-    return ((((me >> 3) + x) & 3) << 3) | ((((me >> 1) + y) & 3) << 1) | ((me + 1 + j) & 1)
-
-
-def stn_peer(me, j):
-    a = j >> 1
-    z = jnp.where((a & 1) == 1, 4 - ((a + 1) >> 1), 4 + (a >> 1))
-    return ((((me >> 3) + 1 + j) & 1) << 3) | ((me + z) & 7)
+def around(step, size):
+    return min(step, size - step)
+
+
+TMPL = sorted(
+    ((x, y, c) for x in range(4) for y in range(4) for c in range(2) if x or y or c),
+    key=lambda d: -(around(d[0], 4) + 2 * around(d[1], 4) + 0.5 * d[2]))
+STN = sorted(
+    ((y, z) for y in range(2) for z in range(8) if y or z), key=lambda d: -(d[0] + around(d[1], 8)))
+
+
+def tmpl_peer(me, by):
+    x, y, c = by
+    return ((((me >> 3) + x) & 3) << 3) | ((((me >> 1) + y) & 3) << 1) | ((me + c) & 1)
+
+
+def stn_peer(me, by):
+    y, z = by
+    return ((((me >> 3) + y) & 1) << 3) | ((me + z) & 7)
 
 
 def kernel(
@@ -76,16 +81,10 @@
 
     bar = pltpu.get_barrier_semaphore()
 
-    def greet_t(j, _):
-        pl.semaphore_signal(bar, inc=1, device_id={"tmpl": tmpl_peer(me_t, j)}, device_id_type=MESH)
-        return 0
-
-    def greet_n(j, _):
-        pl.semaphore_signal(bar, inc=1, device_id={"stn": stn_peer(me_n, j)}, device_id_type=MESH)
-        return 0
-
-    lax.fori_loop(0, NT - 1, greet_t, 0)
-    lax.fori_loop(0, NS - 1, greet_n, 0)
+    for by in sorted(TMPL + STN, key=lambda d: -(
+            around(d[0], 4) + 2 * around(d[1], 4) if len(d) == 3 else d[0] + around(d[1], 8))):
+        to = {"tmpl": tmpl_peer(me_t, by)} if len(by) == 3 else {"stn": stn_peer(me_n, by)}
+        pl.semaphore_signal(bar, inc=1, device_id=to, device_id_type=MESH)
     for copy in small:
         copy.wait()
 
@@ -136,14 +135,11 @@
 
     pl.semaphore_wait(bar, NT - 1 + NS - 1)
 
-    def send_first(j, _):
-        peer = tmpl_peer(me_t, j)
+    for by in TMPL:
+        peer = tmpl_peer(me_t, by)
         pltpu.make_async_remote_copy(
             src_ref=send_a.at[peer], dst_ref=recv_a.at[me_t], send_sem=sa, recv_sem=ra,
             device_id={"tmpl": peer}, device_id_type=MESH).start()
-        return 0
-
-    lax.fori_loop(0, NT - 1, send_first, 0)
 
     large.wait()
 
@@ -234,7 +230,7 @@
                 at = 64 * part + 16 * e
                 vb[sc // 3, at:at + 16, 128 * (sc % 3):128 * (sc % 3) + 128] = y[16 * sc:16 * sc + 16]
 
-    def pair(rr, _):
+    def pair(rr):
         lane16 = iota((16, 128), 1)
         for s2 in range(2):
             s = rr * 2 + s2
@@ -245,13 +241,13 @@
                 z = z0[rr, 16 * (3 * s2 + c):16 * (3 * s2 + c) + 16, :]
                 z1 = next_block(z).astype(bf16)
                 z = z.astype(bf16)
-                lagged = jnp.concatenate([left(x, u) for u in range(12) for x in (z, z1)], axis=0)
-                numer = dot(wt[sc], lagged)
+                lagged = jnp.concatenate([left(x, u) for u in range(11) for x in (z, z1)], axis=0)
+                numer = dot(wt[sc, :, 0:352], lagged)
                 scaled = norm[:, 128 * c:128 * c + 128].reshape(16, 16, 128) * invw[sc][:, None, :]
                 term = numer.reshape(16, 16, 128) * scaled
                 total = term if total is None else total + term
             ssc[s] = total.reshape(256, 128)
-            coarse = pk[pl.ds(pl.multiple_of(16 * s, 16), 16), :] >> 16
+            coarse = pk[16 * s:16 * s + 16, :] >> 16
             for chunk in range(4):
                 merged = None
                 for low in range(4):
@@ -260,27 +256,23 @@
                         x = jnp.where((coarse & (1 << bit)) != 0, left(x, 1 << bit), x)
                     x = left(x, -8 * low)
                     merged = x if merged is None else jnp.where(((lane16 >> 3) & 3) == low, x, merged)
-                aligned[chunk, pl.ds(pl.multiple_of(16 * s, 16), 16), :] = merged
-        return 0
+                aligned[chunk, 16 * s:16 * s + 16, :] = merged
 
     def send(k, which, rows):
         corr = jnp.concatenate(rows, axis=0)
         send_b[k] = dot(pb[which], corr).astype(bf16).reshape(NT, 16, 128)
 
-        def send_second(j, _):
-            peer = tmpl_peer(me_t, j)
+        for by in TMPL:
+            peer = tmpl_peer(me_t, by)
             pltpu.make_async_remote_copy(
                 src_ref=send_b.at[k, peer], dst_ref=recv_b.at[k, me_t], send_sem=sb.at[k], recv_sem=rb.at[k],
                 device_id={"tmpl": peer}, device_id_type=MESH).start()
-            return 0
-
-        for j in range(NT - 1):
-            send_second(j, 0)
         recv_b[k, me_t] = send_b[k, me_t]
 
-    lax.fori_loop(0, 1, pair, 0)
+    pair(0)
     send(0, 0, [aligned[c, 0:32, :] for c in range(4)])
-    lax.fori_loop(1, 3, pair, 0)
+    pair(1)
+    pair(2)
     for k in range(2):
         send(1 + k, 1, [aligned[c, 32:96, :] for c in (2 * k, 2 * k + 1)])
 
@@ -312,14 +304,11 @@
 
     lax.fori_loop(0, NS, onehot, 0)
 
-    def send_counts(j, _):
-        peer = stn_peer(me_n, j)
+    for by in STN:
+        peer = stn_peer(me_n, by)
         pltpu.make_async_remote_copy(
             src_ref=send_k.at[peer], dst_ref=recv_k.at[me_n], send_sem=sk, recv_sem=rk,
             device_id={"stn": peer}, device_id_type=MESH).start()
-        return 0
-
-    lax.fori_loop(0, NS - 1, send_counts, 0)
     recv_k[me_n] = send_k[me_n]
 
     k = iota((512, 512), 1)
@@ -341,15 +330,12 @@
             part = acc[h, rows, :] + dot(ob[2, rows, :], stations)
             send_c[h, pl.ds(y * 8, 8)] = part.astype(bf16).reshape(8, 32, 128)
 
-            def send_stacks(a, _):
-                z = jnp.where((a & 1) == 1, 4 - ((a + 1) >> 1), 4 + (a >> 1))
-                peer = y * 8 + ((me_n + z) & 7)
-                pltpu.make_async_remote_copy(
-                    src_ref=send_c.at[h, peer], dst_ref=recv_c.at[h, me_n], send_sem=sc_.at[h], recv_sem=rc.at[h],
-                    device_id={"stn": peer}, device_id_type=MESH).start()
-                return 0
-
-            lax.fori_loop(0, 7 if i == 1 else 8, send_stacks, 0)
+            for by in STN:
+                if by[0] == 1 - i:
+                    peer = stn_peer(me_n, by)
+                    pltpu.make_async_remote_copy(
+                        src_ref=send_c.at[h, peer], dst_ref=recv_c.at[h, me_n], send_sem=sc_.at[h],
+                        recv_sem=rc.at[h], device_id={"stn": peer}, device_id_type=MESH).start()
         recv_c[h, me_n] = send_c[h, me_n]
 
     pltpu.make_async_copy(send_k.at[pl.ds(0, NS - 1)], recv_k.at[pl.ds(0, NS - 1)], rk).wait()
@@ -358,16 +344,16 @@
     found = found + left(found, 64)
     scale = jnp.sqrt(f32(TAPS)) * lax.rsqrt(jnp.maximum(found, 1.0))
 
-    ordered = []
+    moved = None
     for h in range(2):
         pltpu.make_async_copy(send_c.at[h, pl.ds(0, NS - 1)], recv_c.at[h, pl.ds(0, NS - 1)], rc.at[h]).wait()
         y = jnp.sum(recv_c[h].astype(f32), axis=0)
-        ordered += [y[:16] * scale, y[16:] * scale]
-    y = jnp.concatenate(ordered, axis=1)
-    hi, rest = y.astype(bf16), y - y.astype(bf16).astype(f32)
-    mid, low = split2(rest)
-    moved = dot(jnp.concatenate([hi, mid, low], axis=0), q[...])
-    moved = moved[0:16] + moved[16:32] + moved[32:48]
+        y = jnp.concatenate([y[:16] * scale, y[16:] * scale], axis=1)
+        hi, rest = y.astype(bf16), y - y.astype(bf16).astype(f32)
+        mid, low = split2(rest)
+        three = dot(jnp.concatenate([hi, mid, low], axis=0), q[256 * h:256 * h + 256, :])
+        three = three[0:16] + three[16:32] + three[32:48]
+        moved = three if moved is None else moved + three
     out[0] = moved[:, :256]
     out[1] = moved[:, 256:]
 

time: 45.7 us -> 44.5 us (0.974)
  Pallas kernels: 45 us -> 43.7 us
    pallas_call x1, Pallas kernels: 45 us -> 43.7 us  [body(): pl.pallas_call(kernel, out_shape=pltpu.VMEM((2, 16, 256), f32), in_specs=...]
where the time goes in v4:
time: 44.5 us; the launch traced here: 44.4 us
  Pallas kernels  43.7 us (98%)
  local copies, waits for them, and re-layouts  0.62 us (1%)
    pallas_call x1, Pallas kernels, body(): pl.pallas_call(kernel, out_shape=pltpu.VMEM((2, 16, 256), f32), in_specs=...  43.7 us

profile of v4, /device:TPU:1, one launch (start us, length us, event | category | flops | bytes accessed | tf_op | source)
XLA Modules:
  0.0 44.4 jit_solution(15314724103962057081)
XLA Ops:
  0.0 43.7 %shard_map.64 = f32[2,16,256]{2,1,0:T(8,128)S(1)} custom-call(bf16[18,2,32]{2,1,0:T(2,128)(2,1)} %bitcast.9, bf16[18,16,300]{2,1,0:T(8,128)(2,1)} %bitcast.8, s32[6,1,16]{2,1,0:T(1,128)} %bitcast.10, s32[6,16]{1,0:T(8,128)} %local_in.1, s32[6,16]{1,0:T(8,128)} %move_in.1, s32[3,6]{1,0:T(4,128)} %bitcast.11), custom_call_target="tpu_custom_call" | custom-call | tf_op jit(solution)/shard_map/pallas_call | solution.py:372
  43.7 0.6 %copy.8 = f32[2,16,256]{2,1,0:T(8,128)} copy(f32[2,16,256]{2,1,0:T(8,128)S(1)} %shard_map.64) | data formatting | bytes 65536

commit v5 on v4

--- a/solution.py
+++ b/solution.py
@@ -297,9 +297,9 @@
             hit = jnp.where(code[:32] == key[4 + u:5 + u, :], 1.0, 0.0)
             ob[2, rows, at] = hit.astype(bf16)
             found = found + hit[:16]
-        number = jnp.broadcast_to(jnp.sum(found, axis=1, keepdims=True), (16, 128)).astype(i32)
-        parts = jnp.where(iota((16, 128), 1) < 64, number & 127, number >> 7)
-        send_k[n] = parts.astype(f32).astype(bf16)
+        number = jnp.sum(found, axis=1, keepdims=True)
+        along = jnp.where(iota((16, 128), 0) == iota((16, 128), 1), number, 0.0)
+        send_k[n, 0:1, :] = jnp.sum(along, axis=0, keepdims=True)
         return 0
 
     lax.fori_loop(0, NS, onehot, 0)
@@ -307,9 +307,9 @@
     for by in STN:
         peer = stn_peer(me_n, by)
         pltpu.make_async_remote_copy(
-            src_ref=send_k.at[peer], dst_ref=recv_k.at[me_n], send_sem=sk, recv_sem=rk,
+            src_ref=send_k.at[peer, pl.ds(0, 1)], dst_ref=recv_k.at[me_n, pl.ds(0, 1)], send_sem=sk, recv_sem=rk,
             device_id={"stn": peer}, device_id_type=MESH).start()
-    recv_k[me_n] = send_k[me_n]
+    recv_k[me_n, 0:1, :] = send_k[me_n, 0:1, :]
 
     k = iota((512, 512), 1)
     place = ((k >> 2) & 3) * 128 + (k >> 8) * 64 + ((k >> 4) & 1) * 32 + (k & 3) * 8 + ((k >> 5) & 7)
@@ -338,10 +338,10 @@
                         recv_sem=rc.at[h], device_id={"stn": peer}, device_id_type=MESH).start()
         recv_c[h, me_n] = send_c[h, me_n]
 
-    pltpu.make_async_copy(send_k.at[pl.ds(0, NS - 1)], recv_k.at[pl.ds(0, NS - 1)], rk).wait()
-    found = jnp.sum(recv_k[...].astype(f32), axis=0)
-    found = jnp.where(iota((16, 128), 1) < 64, found, found * 128.0)
-    found = found + left(found, 64)
+    pltpu.make_async_copy(send_k.at[pl.ds(0, NS - 1), pl.ds(0, 1)], recv_k.at[pl.ds(0, NS - 1), pl.ds(0, 1)], rk).wait()
+    found = jnp.broadcast_to(jnp.sum(recv_k[:, 0:1, :], axis=0), (16, 128))
+    found = jnp.where(iota((16, 128), 0) == iota((16, 128), 1), found, 0.0)
+    found = jnp.broadcast_to(jnp.sum(found, axis=1, keepdims=True), (16, 128))
     scale = jnp.sqrt(f32(TAPS)) * lax.rsqrt(jnp.maximum(found, 1.0))
 
     moved = None
@@ -360,7 +360,7 @@
     pltpu.make_async_copy(send_a.at[pl.ds(0, NT - 1)], recv_a.at[pl.ds(0, NT - 1)], sa).wait()
     for rr in range(3):
         pltpu.make_async_copy(send_b.at[rr, pl.ds(0, NT - 1)], recv_b.at[rr, pl.ds(0, NT - 1)], sb.at[rr]).wait()
-    pltpu.make_async_copy(send_k.at[pl.ds(0, NS - 1)], recv_k.at[pl.ds(0, NS - 1)], sk).wait()
+    pltpu.make_async_copy(send_k.at[pl.ds(0, NS - 1), pl.ds(0, 1)], recv_k.at[pl.ds(0, NS - 1), pl.ds(0, 1)], sk).wait()
     for h in range(2):
         pltpu.make_async_copy(send_c.at[h, pl.ds(0, NS - 1)], recv_c.at[h, pl.ds(0, NS - 1)], sc_.at[h]).wait()
 
@@ -402,8 +402,8 @@
             pltpu.VMEM((2, 512, 128), f32),
             pltpu.VMEM((2, NS, 32, 128), bf16),
             pltpu.VMEM((2, NS, 32, 128), bf16),
-            pltpu.VMEM((NS, 16, 128), bf16),
-            pltpu.VMEM((NS, 16, 128), bf16),
+            pltpu.VMEM((NS, 8, 128), f32),
+            pltpu.VMEM((NS, 8, 128), f32),
             pltpu.VMEM((512, 512), bf16),
             dma((5,)), dma, dma, dma, dma((3,)), dma((3,)), dma((2,)), dma((2,)), dma, dma,
         ],

time: 44.5 us -> 44.5 us (level)
  no operation moved by 1% of the time
where the time goes in v5:
time: 44.5 us; the launch traced here: 44.3 us
  Pallas kernels  43.7 us (98%)
  local copies, waits for them, and re-layouts  0.62 us (1%)
    pallas_call x1, Pallas kernels, body(): pl.pallas_call(kernel, out_shape=pltpu.VMEM((2, 16, 256), f32), in_specs=...  43.7 us

profile of v5, /device:TPU:1, one launch (start us, length us, event | category | flops | bytes accessed | tf_op | source)
XLA Modules:
  0.0 44.3 jit_solution(11608752134406857887)
XLA Ops:
  0.0 43.7 %shard_map.64 = f32[2,16,256]{2,1,0:T(8,128)S(1)} custom-call(bf16[18,2,32]{2,1,0:T(2,128)(2,1)} %bitcast.9, bf16[18,16,300]{2,1,0:T(8,128)(2,1)} %bitcast.8, s32[6,1,16]{2,1,0:T(1,128)} %bitcast.10, s32[6,16]{1,0:T(8,128)} %local_in.1, s32[6,16]{1,0:T(8,128)} %move_in.1, s32[3,6]{1,0:T(4,128)} %bitcast.11), custom_call_target="tpu_custom_call" | custom-call | tf_op jit(solution)/shard_map/pallas_call | solution.py:372
  43.7 0.6 %copy.8 = f32[2,16,256]{2,1,0:T(8,128)} copy(f32[2,16,256]{2,1,0:T(8,128)S(1)} %shard_map.64) | data formatting | bytes 65536
